TPU v7x, 32 devices: a whole 2x2x4 slice. The times are simulated.
32 devices in a mesh: dp: 2 (over x), expert: 4 (over z), mp: 4 (over y, core).
Axes of the slice: x: 2, y: 2, z: 4, core: 2. Of those that a mesh axis runs over, the one named last changes fastest.
Arguments:
- tokens: bfloat16 [1024, 3072], P(('dp', 'expert'), 'mp'), may hold values from -6 to 6
- expert_ids: int32 [1024, 2], P(('dp', 'expert')), may hold values from 0 to 3, all different within a row; in each aligned block of 128 rows (0 to 127, 128 to 255, ...) at most 72 rows name the same one
- route_weight: bfloat16 [1024, 2], P(('dp', 'expert')), may hold values from 0.099609375 to 1
- w_gate: bfloat16 [4, 3072, 8192], P(None, ('dp', 'expert'), 'mp'), may hold values from -0.109375 to 0.109375
- w_up: bfloat16 [4, 3072, 8192], P(None, ('dp', 'expert'), 'mp'), may hold values from -0.109375 to 0.109375
- grad_hidden: bfloat16 [4, 2, 4, 72, 8192], P('expert', 'dp', None, None, 'mp'), may hold values from -6 to 6
Outputs:
- hidden_out: bfloat16 [4, 2, 4, 72, 8192], P('expert', 'dp', None, None, 'mp')
- grad_tokens: bfloat16 [1024, 3072], P(('dp', 'expert'), 'mp')
Inputs may be any that keep to these rules, and one draw needn't show every extreme that they name: `expert_ids`: each row names 2 different experts; among the rows of one token group no expert is named more than 72 times, a bound that some block reaches.
All inputs are finite; a program needn't handle non-finite values.
Results may differ from a plain program's by a relative error of at most 0.0049.
Values may be sent and summed in bfloat16 or wider, within the bound.
No kernel may reach another device: no remote copies, remote signals or barrier semaphores. Data moves between devices by JAX's collectives and lax.ppermute only.
A program may use at most 128 MiB of HBM per device.

v0:
```python
import jax
import jax.numpy as jnp
from jax import lax
from jax.sharding import PartitionSpec as P

D = 3072


def slot_map(expert_ids, n_expert, slots_cap):
    flat_ids = expert_ids.reshape(-1)
    onehot = (flat_ids[:, None] == jnp.arange(n_expert, dtype=jnp.int32)[None, :]).astype(jnp.int32)
    before = jnp.cumsum(onehot, axis=0) - onehot
    position = jnp.sum(before * onehot, axis=1)
    target = flat_ids * slots_cap + position
    placed = target[:, None] == jnp.arange(n_expert * slots_cap, dtype=jnp.int32)[None, :]
    return placed.reshape(expert_ids.shape[0], expert_ids.shape[1], n_expert * slots_cap)


def per_device(tokens, expert_ids, route_weight, w_gate, w_up, grad_hidden):
    n_expert = lax.axis_size("expert")
    slots_cap = grad_hidden.shape[3]
    feat_part = tokens.shape[1]
    hidden_part = w_gate.shape[2]
    slot_count = n_expert * slots_cap
    placed = slot_map(expert_ids, n_expert, slots_cap).astype(jnp.float32)
    select = jnp.sum(placed, axis=1)
    sent_rows = jnp.dot(
        select.T.astype(jnp.bfloat16), tokens, preferred_element_type=jnp.float32
    ).astype(jnp.bfloat16)
    sent_scale = jnp.einsum(
        "tks,tk->s", placed, route_weight.astype(jnp.float32), precision=lax.Precision.HIGHEST
    ).astype(jnp.bfloat16)
    recv_rows, recv_scale = (
        lax.all_to_all(
            sent_rows.reshape(n_expert, slots_cap, feat_part),
            "expert",
            split_axis=0,
            concat_axis=0,
            tiled=True,
        ),
        lax.all_to_all(
            sent_scale.reshape(n_expert, slots_cap),
            "expert",
            split_axis=0,
            concat_axis=0,
            tiled=True,
        ),
    )
    rows_full = lax.all_gather(recv_rows, "mp", axis=2, tiled=True).reshape(slot_count, D)
    owned_gate, owned_up = (
        lax.all_to_all(w_gate, "expert", split_axis=0, concat_axis=1, tiled=True),
        lax.all_to_all(w_up, "expert", split_axis=0, concat_axis=1, tiled=True),
    )
    piece_gate = lax.all_gather(owned_gate, "dp", axis=1, tiled=True)[0]
    piece_up = lax.all_gather(owned_up, "dp", axis=1, tiled=True)[0]
    gate_acc = jnp.dot(rows_full, piece_gate, preferred_element_type=jnp.float32)
    up_acc = jnp.dot(rows_full, piece_up, preferred_element_type=jnp.float32)
    weight = recv_scale.reshape(slot_count).astype(jnp.float32)[:, None]
    sigmoid_gate = jax.nn.sigmoid(gate_acc)
    hidden = (weight * gate_acc * sigmoid_gate * up_acc).astype(jnp.bfloat16)
    grad_act = weight * grad_hidden.reshape(slot_count, hidden_part).astype(jnp.float32)
    gate_grad = (grad_act * up_acc * sigmoid_gate * (1.0 + gate_acc * (1.0 - sigmoid_gate))).astype(
        jnp.bfloat16
    )
    up_grad = (grad_act * gate_acc * sigmoid_gate).astype(jnp.bfloat16)
    dims = (((1,), (1,)), ((), ()))
    back_term = lax.dot_general(gate_grad, piece_gate, dims, preferred_element_type=jnp.float32)
    back_term = back_term + lax.dot_general(
        up_grad, piece_up, dims, preferred_element_type=jnp.float32
    )
    shared = lax.psum_scatter(
        back_term.reshape(n_expert, slots_cap, D), "mp", scatter_dimension=2, tiled=True
    )
    returned = lax.all_to_all(shared, "expert", split_axis=0, concat_axis=0, tiled=True)
    grad_tokens = jnp.dot(
        select, returned.reshape(slot_count, feat_part), precision=lax.Precision.HIGHEST
    )
    hidden_out = hidden.reshape(1, 1, n_expert, slots_cap, hidden_part)
    return (hidden_out, grad_tokens.astype(jnp.bfloat16))


def solution(mesh):
    in_specs = (
        P(("dp", "expert"), "mp"),
        P(("dp", "expert"), None),
        P(("dp", "expert"), None),
        P(None, ("dp", "expert"), "mp"),
        P(None, ("dp", "expert"), "mp"),
        P("expert", "dp", None, None, "mp"),
    )
    out_specs = (P("expert", "dp", None, None, "mp"), P(("dp", "expert"), "mp"))
    return jax.shard_map(
        per_device, mesh=mesh, in_specs=in_specs, out_specs=out_specs, check_vma=False
    )
```

profile of v0, /device:TPU:0, one launch (start us, length us, event | category | flops | bytes accessed | tf_op | source)
XLA Modules:
  0.0 588.8 jit_solution(11257761073279817693)
XLA Ops:
  7.2 0.0 copy-start
  7.2 0.8 copy.32
  8.0 0.1 eq.43
  8.1 0.1 eq.39
  8.3 1.2 reduce-window.6
  9.5 0.1 slice.8
  9.6 0.1 copy.34
  9.7 0.1 copy.35
  9.8 0.1 add_bitcast_fusion
  9.9 0.1 reduce_sum.21
  10.1 0.1 copy.36
  10.1 0.7 multiply_add_fusion
  10.9 0.0 copy-done
  10.9 0.3 convolution_convert_fusion
  11.2 19.0 %all_to_all.44 = bf16[4,72,768]{2,1,0:T(8,128)(2,1)} all-to-all(bf16[4,72,768]{2,1,0:T(8,128)(2,1)S(1)} %bitcast.51), channel_id=1, replica_groups=mesh['dp'=2,'expert'=4,'mp'=4] {'expert'}, dimensions={0} | all-to-all | bytes 884736 | tf_op jit(solution)/shard_map/all_to_all | solution.py:34
  30.1 5.2 all-to-all-start.2
  35.4 0.0 all-gather.4.cloned.1.call-start
  35.4 0.7 all-gather.4.cloned.1.call-update
  36.1 0.0 all-gather.6.cloned.1.call-start
  36.1 136.8 %all-to-all-done.2 = bf16[4,384,2048]{2,1,0:T(8,128)(2,1)} async-done(((bf16[4,384,2048]{2,1,0:T(8,128)(2,1)}), bf16[4,384,2048]{2,1,0:T(8,128)(2,1)}, u32[]{:S(2)}, u32[]{:S(2)}) %all-to-all-start.2) | async-done | bytes 6291488 | tf_op jit(solution)/shard_map/all_to_all | solution.py:51
  172.9 0.0 all-gather.6.cloned.1.call-update
  173.0 0.0 all-gather.8.cloned.1.call-start
  173.0 144.5 %all_to_all.45 = bf16[4,384,2048]{2,1,0:T(8,128)(2,1)} all-to-all(bf16[4,384,2048]{2,1,0:T(8,128)(2,1)} %param.10), channel_id=1, replica_groups=mesh['dp'=2,'expert'=4,'mp'=4] {'expert'}, dimensions={0} | all-to-all | bytes 12582912 | tf_op jit(solution)/shard_map/all_to_all | solution.py:52
  317.5 0.0 copy-start.4
  317.5 0.0 all-gather.8.cloned.1.call-update
  317.6 0.0 reduce-scatter.2.cloned.1.call-start
  317.6 0.6 copy-done.4
  318.2 0.2 convolution_reduce_fusion
  318.4 0.1 all_to_all.38
  318.5 7.9 %all_to_all.46 = bf16[4,1,72]{2,1,0:T(2,128)(2,1)S(1)} all-to-all(bf16[4,1,72]{2,1,0:T(2,128)(2,1)S(1)} %all_to_all.38), channel_id=1, replica_groups=mesh['dp'=2,'expert'=4,'mp'=4] {'expert'}, dimensions={0} | all-to-all | bytes 1152 | tf_op jit(solution)/shard_map/all_to_all | solution.py:41
  326.4 0.1 reshape.82
  326.5 0.0 all-gather.6.cloned.1.call-done
  326.5 10.7 %fusion.6 = f32[288,2048]{1,0:T(8,128)} fusion(bf16[288,3072]{1,0:T(8,128)(2,1)} %bitcast.53, bf16[1,3072,2048]{2,1,0:T(8,128)(2,1)} %all-gather.6.cloned.1.call-done), kind=kOutput, calls=%fused_computation.6 | convolution fusion | flops 3623878656 | bytes 16711680 | tf_op jit(solution)/shard_map/dot_general | solution.py:56
  337.2 141.7 %all-gather.8.cloned.1.call-done = bf16[1,3072,2048]{2,1,0:T(8,128)(2,1)} async-done(((bf16[1,1536,2048]{2,1,0:T(8,128)(2,1)}), bf16[1,3072,2048]{2,1,0:T(8,128)(2,1)}) %all-gather.8.cloned.1.call-update) | async-done | bytes 12582928 | tf_op jit(solution)/shard_map/all_gather | solution.py:55
  478.9 0.0 copy-done.2
  478.9 10.7 %multiply_convert_fusion = (bf16[288,2048]{1,0:T(8,128)(2,1)}, f32[288,2048]{1,0:T(8,128)}) fusion(f32[288,2048]{1,0:T(8,128)} %fusion.6, f32[288]{0:T(512)S(1)} %reshape.82, bf16[288,3072]{1,0:T(8,128)(2,1)S(1)} %bitcast.54, bf16[1,3072,2048]{2,1,0:T(8,128)(2,1)} %all-gather.8.cloned.1.call-done), kind=kOutput, calls=%fused_computation.17 | convolution fusion | flops 3628007424 | bytes 20251776 | tf_op jit(solution)/shard_map/dot_general | solution.py:57
  489.6 0.0 copy-done.3
  489.6 0.0 copy-done.5
  489.6 0.0 copy-start.6
  489.6 10.9 %fusion = f32[288,3072]{1,0:T(8,128)} fusion(bf16[1,3072,2048]{2,1,0:T(8,128)(2,1)} %all-gather.8.cloned.1.call-done, f32[288,2048]{1,0:T(8,128)S(1)} %copy-done.5, bf16[288,2048]{1,0:T(8,128)(2,1)S(1)} %bitcast.55, f32[288]{0:T(512)S(1)} %reshape.82), kind=kOutput, calls=%fused_computation | convolution fusion | flops 3628597248 | bytes 19661952 | tf_op jit(solution)/shard_map/dot_general | solution.py:68
  500.5 0.0 copy-done.6
  500.5 12.8 %fusion.8 = f32[288,3072]{1,0:T(8,128)} fusion(f32[288,3072]{1,0:T(8,128)} %fusion, bf16[1,3072,2048]{2,1,0:T(8,128)(2,1)} %all-gather.6.cloned.1.call-done, f32[288,2048]{1,0:T(8,128)} %get-tuple-element.3, bf16[288,2048]{1,0:T(8,128)(2,1)S(1)} %bitcast.56, f32[288,2048]{1,0:T(8,128)S(1)} %copy-done.6, f32[288]{0:T(512)S(1)} %reshape.82), kind=kOutput, calls=%fused_computation.8 | convolution fusion | flops 3631841280 | bytes 25560192 | tf_op jit(solution)/shard_map/dot_general | solution.py:67
  513.3 0.0 reduce-scatter.2.cloned.1.call-update
  513.3 0.0 copy-start.1
  513.3 40.6 %reduce-scatter.2.cloned.1.call-done = f32[4,72,768]{2,1,0:T(8,128)} async-done(((f32[4,72,3072]{2,1,0:T(8,128)}), f32[4,72,768]{2,1,0:T(8,128)}) %reduce-scatter.2.cloned.1.call-update) | async-done | bytes 884752 | tf_op jit(solution)/shard_map/reduce_scatter | solution.py:71
  553.9 26.8 %all_to_all.47 = f32[4,72,768]{2,1,0:T(8,128)S(1)} all-to-all(f32[4,72,768]{2,1,0:T(8,128)} %reduce-scatter.2.cloned.1.call-done), channel_id=1, replica_groups=mesh['dp'=2,'expert'=4,'mp'=4] {'expert'}, dimensions={0} | all-to-all | bytes 1769472 | tf_op jit(solution)/shard_map/all_to_all | solution.py:74
  580.7 1.5 convolution_convert_fusion.1
  582.2 0.0 copy-done.1
  (10 shorter events, 0.1 us)
Async XLA Ops:
  7.2 3.7 copy-start
  30.1 142.8 %all-to-all-start.2 = ((bf16[4,384,2048]{2,1,0:T(8,128)(2,1)}), bf16[4,384,2048]{2,1,0:T(8,128)(2,1)}, u32[]{:S(2)}, u32[]{:S(2)}) async-start(bf16[4,384,2048]{2,1,0:T(8,128)(2,1)} %param.9), calls=%async_computation.2 | async-start | bytes 12582912 | tf_op jit(solution)/shard_map/all_to_all | solution.py:51
  35.4 291.1 %all-gather.4.cloned.1.call-start = ((), (), s32[]{:S(2)}) async-start(), calls=%async_computation.6 | async-start | bytes 2211840 | tf_op jit(solution)/shard_map/all_gather | solution.py:49
  36.1 290.4 %all-gather.6.cloned.1.call-start = ((), (), s32[]{:S(2)}) async-start(), calls=%async_computation.7 | async-start | bytes 18874368 | tf_op jit(solution)/shard_map/all_gather | solution.py:54
  173.0 305.9 %all-gather.8.cloned.1.call-start = ((), (), s32[]{:S(2)}) async-start(), calls=%async_computation.8 | async-start | bytes 18874368 | tf_op jit(solution)/shard_map/all_gather | solution.py:55
  317.5 0.7 copy-start.4
  317.6 236.3 %reduce-scatter.2.cloned.1.call-start = ((), (), s32[]{:S(2)}) async-start(), calls=%async_computation.9 | async-start | bytes 4423680 | tf_op jit(solution)/shard_map/reduce_scatter | solution.py:71
  326.5 152.4 %copy-start.2 = (bf16[4,72,3072]{2,1,0:T(8,128)(2,1)S(1)}, bf16[4,72,3072]{2,1,0:T(8,128)(2,1)}, u32[]{:S(2)}) copy-start(bf16[4,72,3072]{2,1,0:T(8,128)(2,1)} %all-gather.4.cloned.1.call-done) | copy-start | bytes 5308420
  337.2 152.4 %copy-start.3 = (bf16[1,1,4,72,2048]{4,3,2,1,0:T(8,128)(2,1)S(1)}, bf16[1,1,4,72,2048]{4,3,2,1,0:T(8,128)(2,1)}, u32[]{:S(2)}) copy-start(bf16[1,1,4,72,2048]{4,3,2,1,0:T(8,128)(2,1)} %param.11) | copy-start | bytes 3538948
  478.9 10.7 %copy-start.5 = (f32[288,2048]{1,0:T(8,128)S(1)}, f32[288,2048]{1,0:T(8,128)}, u32[]{:S(2)}) copy-start(f32[288,2048]{1,0:T(8,128)} %fusion.6) | copy-start | bytes 7077892
  489.6 10.9 %copy-start.6 = (f32[288,2048]{1,0:T(8,128)S(1)}, f32[288,2048]{1,0:T(8,128)}, u32[]{:S(2)}) copy-start(f32[288,2048]{1,0:T(8,128)} %fusion.6) | copy-start | bytes 7077892
  513.3 68.9 %copy-start.1 = (bf16[128,768]{1,0:T(8,128)(2,1)S(1)}, bf16[128,768]{1,0:T(8,128)(2,1)}, u32[]{:S(2)}) copy-start(bf16[128,768]{1,0:T(8,128)(2,1)} %param.6) | copy-start | bytes 589828
Sparse Core Ops, SparseCore 0:
  37.8 22.1 all-gather.3
  173.1 151.6 all-gather.5
  326.3 152.5 all-gather.7
  513.4 40.4 reduce-scatter.1
where the time goes:
time: 589 us
  waiting for transfers between devices  320 us (54%)
  blocking collectives  198 us (34%)
  matrix products  47.1 us (8%)
  between operations  13.9 us (2%)
    all_to_all x1, blocking collectives, per_device(): lax.all_to_all(w_up, 'expert', split_axis=0, concat_axis=1, tiled=True)  145 us
    all_gather x1, waiting for transfers between devices, per_device(): piece_up = lax.all_gather(owned_up, 'dp', axis=1, tiled=True)[0]  142 us
    all_to_all x1, waiting for transfers between devices, per_device(): lax.all_to_all(w_gate, 'expert', split_axis=0, concat_axis=1, tiled=True)  137 us
    reduce_scatter x1, waiting for transfers between devices, per_device(): lax.psum_scatter(back_term.reshape(n_expert, slots_cap, D), 'mp', scatter...  40.6 us
    all_to_all x1, blocking collectives, per_device(): lax.all_to_all(shared, 'expert', split_axis=0, concat_axis=0, tiled=True)  26.8 us
    all_to_all x1, blocking collectives, per_device(): lax.all_to_all(sent_rows.reshape(n_expert, slots_cap, feat_part), 'expert...  19 us
    dot_general x1, matrix products, per_device(): lax.dot_general(gate_grad, piece_gate, dims, preferred_element_type=jnp.f...  12.8 us
  transfers between devices with their start and end apart: 5, of which 3 were waited for; matrix products, arithmetic and copies ran while one was open for 2% of the time, Pallas kernels for 0%

commit v1 on v0

v1 whole, which is shorter than its diff:
```python
import functools

import jax
import jax.numpy as jnp
from jax import lax
from jax.experimental import pallas as pl
from jax.experimental.pallas import tpu as pltpu
from jax.sharding import PartitionSpec as P

Z_WINDOW = 3
X_WINDOW = 3
Z_LAG = 3
X_LAG = 2
OWN_AT = (0, 0, 0, 1, 2, 3, 4, 5)
NT = (((1,), (1,)), ((), ()))


def slot_map(expert_ids, n_expert, slots_cap):
    flat_ids = expert_ids.reshape(-1)
    onehot = (flat_ids[:, None] == jnp.arange(n_expert, dtype=jnp.int32)[None, :]).astype(jnp.int32)
    before = jnp.cumsum(onehot, axis=0) - onehot
    position = jnp.sum(before * onehot, axis=1)
    target = flat_ids * slots_cap + position
    placed = target[:, None] == jnp.arange(n_expert * slots_cap, dtype=jnp.int32)[None, :]
    return placed.reshape(expert_ids.shape[0], expert_ids.shape[1], n_expert * slots_cap)


def shift_by(axis, step):
    size = lax.axis_size(axis)
    return [(source, (source + step) % size) for source in range(size)]


def exchange(axis, bit):
    return [(source, source ^ bit) for source in range(lax.axis_size(axis))]


def after(value, *others):
    return lax.optimization_barrier((value, *others))[0]


def column_chunks(width):
    unit = width // 16
    sizes = (2, 4, 4, 4, 2)
    bounds = [0]
    for size in sizes:
        bounds.append(bounds[-1] + size * unit)
    return list(zip(bounds[:-1], bounds[1:]))


def expert_kernel(n_part, first, rows_ref, scale_ref, grad_ref, *refs):
    parts, rest = refs[:n_part], refs[n_part:]
    if first:
        hidden_ref, back_ref, done_ref = rest
    else:
        back_in, _, hidden_ref, back_ref, done_ref = rest
    depth = parts[0].shape[1]

    @pl.when(pl.program_id(0) == 0)
    def _():
        if first:
            back_ref[...] = jnp.zeros_like(back_ref)
        else:
            back_ref[...] = back_in[...]
        done_ref[...] = jnp.zeros_like(done_ref)

    gate = up = None
    for index, part in enumerate(parts):
        rows = rows_ref[:, index * depth : (index + 1) * depth]
        gate_term = jnp.dot(rows, part[0], preferred_element_type=jnp.float32)
        up_term = jnp.dot(rows, part[1], preferred_element_type=jnp.float32)
        gate = gate_term if gate is None else gate + gate_term
        up = up_term if up is None else up + up_term
    weight = scale_ref[...]
    sig = jax.nn.sigmoid(gate)
    hidden_ref[...] = (weight * gate * sig * up).astype(jnp.bfloat16)
    grad_act = weight * grad_ref[...].astype(jnp.float32)
    gate_grad = (grad_act * up * sig * (1.0 + gate * (1.0 - sig))).astype(jnp.bfloat16)
    up_grad = (grad_act * gate * sig).astype(jnp.bfloat16)
    for index, part in enumerate(parts):
        columns = slice(index * depth, (index + 1) * depth)
        back_ref[:, columns] += lax.dot_general(
            gate_grad, part[0], NT, preferred_element_type=jnp.float32
        ) + lax.dot_general(up_grad, part[1], NT, preferred_element_type=jnp.float32)


def expert_chunk(rows, scale, grad, parts, begin, carried):
    slot_count, width_all = rows.shape
    hidden_part = grad.shape[1]
    depth, width = parts[0].shape[1:]
    tile = 256 if width % 256 == 0 and begin % 256 == 0 else 128
    tile = tile if width % tile == 0 else width
    offset = begin // tile
    whole = lambda shape: pl.BlockSpec(shape, lambda t: (0, 0))
    columns = pl.BlockSpec((slot_count, tile), lambda t: (0, offset + t))
    in_specs = [whole((slot_count, width_all)), whole((slot_count, 1)), columns]
    in_specs += [pl.BlockSpec((2, depth, tile), lambda t: (0, 0, t))] * len(parts)
    operands = [rows, scale, grad, *parts]
    aliases = {}
    if carried is not None:
        hidden, back = carried
        in_specs += [whole((slot_count, width_all)), pl.BlockSpec(memory_space=pl.ANY)]
        aliases = {len(operands): 1, len(operands) + 1: 0}
        operands += [back, hidden]
    return pl.pallas_call(
        functools.partial(expert_kernel, len(parts), carried is None),
        grid=(width // tile,),
        out_shape=(
            jax.ShapeDtypeStruct((slot_count, hidden_part), jnp.bfloat16),
            jax.ShapeDtypeStruct((slot_count, width_all), jnp.float32),
            jax.ShapeDtypeStruct((8, 128), jnp.float32),
        ),
        in_specs=in_specs,
        out_specs=(columns, whole((slot_count, width_all)), whole((8, 128))),
        input_output_aliases=aliases,
        compiler_params=pltpu.CompilerParams(vmem_limit_bytes=48 * 1024 * 1024),
        cost_estimate=pl.CostEstimate(
            flops=8 * slot_count * width_all * width,
            bytes_accessed=4 * width_all * width + 10 * slot_count * width_all,
            transcendentals=slot_count * width,
        ),
    )(*operands)


def per_device(tokens, expert_ids, route_weight, w_gate, w_up, grad_hidden):
    n_expert = lax.axis_size("expert")
    n_dp = lax.axis_size("dp")
    n_mp = lax.axis_size("mp")
    my_expert = lax.axis_index("expert")
    my_dp = lax.axis_index("dp")
    my_mp = lax.axis_index("mp")
    slots_cap = grad_hidden.shape[3]
    feat_part = tokens.shape[1]
    depth = w_gate.shape[1]
    hidden_part = w_gate.shape[2]
    slot_count = n_expert * slots_cap
    width_all = n_expert * n_dp * depth
    chunks = column_chunks(hidden_part)
    pair = n_dp == 2

    def stored(chunk, step):
        begin, end = chunks[chunk]
        target = lax.rem(my_expert + step, n_expert)
        return jnp.stack(
            [
                lax.dynamic_slice(w, (target, 0, begin), (1, depth, end - begin))[0]
                for w in (w_gate, w_up)
            ]
        )

    shifts = sorted(range(1, n_expert), key=lambda s: -abs(2 * s - n_expert))
    landed, arrivals = {}, []
    spread, crossings = {}, []
    carried, finished = None, []

    def to_owner(chunk, step):
        piece = stored(chunk, step)
        if step:
            first = [arrivals[-Z_WINDOW]] if len(arrivals) >= Z_WINDOW else []
            if chunk >= Z_LAG:
                first.append(finished[chunk - Z_LAG])
            if first:
                piece = after(piece, *first)
            piece = lax.ppermute(piece, "expert", shift_by("expert", step))
            arrivals.append(piece)
        landed[chunk, step] = piece

    def to_both(chunk, step):
        piece = landed[chunk, step]
        first = [crossings[-X_WINDOW]] if len(crossings) >= X_WINDOW else []
        if step and chunk >= X_LAG:
            first.append(finished[chunk - X_LAG])
        if first:
            piece = after(piece, *first)
        if pair:
            spread[chunk, step] = lax.ppermute(piece, "dp", shift_by("dp", 1))
        else:
            spread[chunk, step] = lax.all_gather(piece, "dp", axis=1, tiled=True)
        crossings.append(spread[chunk, step])

    to_owner(0, 0)
    for step in shifts:
        to_owner(0, step)
    to_both(0, 0)

    def place_of(dp_index, expert_index):
        step = lax.rem(my_expert - expert_index + n_expert, n_expert)
        far = lax.rem(my_dp - dp_index + n_dp, n_dp) if pair else dp_index
        return (step * n_dp + far) * depth

    order = []
    for step in range(n_expert):
        expert_index = lax.rem(my_expert - step + n_expert, n_expert)
        for far in range(n_dp):
            dp_index = lax.rem(my_dp - far + n_dp, n_dp) if pair else far
            order.append((dp_index * n_expert + expert_index) * depth)

    expert_ids = after(expert_ids, landed[0, 0])
    placed = slot_map(expert_ids, n_expert, slots_cap).astype(jnp.float32)
    select = jnp.sum(placed, axis=1)
    sent_rows = jnp.dot(
        select.T.astype(jnp.bfloat16), tokens, preferred_element_type=jnp.float32
    ).astype(jnp.bfloat16)
    sent_scale = jnp.einsum(
        "tks,tk->s", placed, route_weight.astype(jnp.float32), precision=lax.Precision.HIGHEST
    ).astype(jnp.bfloat16)
    sent = jnp.concatenate(
        [sent_rows, jnp.broadcast_to(sent_scale[:, None], (slot_count, 128))], axis=1
    ).reshape(n_expert, slots_cap, feat_part + 128)
    came = []
    for step in range(n_expert):
        block = lax.dynamic_index_in_dim(sent, lax.rem(my_expert + step, n_expert), 0, keepdims=False)
        came.append(lax.ppermute(block, "expert", shift_by("expert", step)) if step else block)
    came = jnp.stack(came)
    slots = jnp.concatenate(
        [
            lax.dynamic_index_in_dim(came, lax.rem(my_expert - group + n_expert, n_expert), 0, keepdims=False)
            for group in range(n_expert)
        ],
        axis=0,
    )
    scale = slots[:, feat_part : feat_part + 1].astype(jnp.float32)
    rows_full = lax.all_gather(slots[:, :feat_part], "mp", axis=1, tiled=True)
    rows = jnp.concatenate(
        [lax.dynamic_slice(rows_full, (0, start), (slot_count, depth)) for start in order], axis=1
    )
    grad_rows = grad_hidden.reshape(slot_count, hidden_part)

    n_chunk = len(chunks)
    own_at = OWN_AT
    for chunk in range(n_chunk):
        for later in range(1, n_chunk):
            if own_at[later] == chunk:
                to_owner(later, 0)
                to_both(later, 0)
        if chunk:
            for step in shifts:
                to_owner(chunk, step)
        for step in shifts:
            to_both(chunk, step)
        parts = []
        for step in range(n_expert):
            parts += [landed[chunk, step], spread[chunk, step]] if pair else [spread[chunk, step]]
        *carried, done = expert_chunk(rows, scale, grad_rows, parts, chunks[chunk][0], carried)
        finished.append(done)
    hidden, back = carried

    blocks_per_part = feat_part // depth

    def features(part_index):
        blocks = []
        for block in range(blocks_per_part):
            number = part_index * blocks_per_part + block
            start = place_of(number // n_expert, lax.rem(number, n_expert))
            blocks.append(lax.dynamic_slice(back, (0, start), (slot_count, depth)))
        return jnp.concatenate(blocks, axis=1)

    sums = {bits: features(my_mp ^ bits) for bits in range(n_mp)}
    bit = 1
    while 2 * bit < n_mp:
        going = [bits for bits in sums if bits & bit]
        got = lax.ppermute(jnp.stack([sums[bits] for bits in going]), "mp", exchange("mp", bit))
        for index, bits in enumerate(going):
            sums[bits ^ bit] = sums[bits ^ bit] + got[index]
            del sums[bits]
        bit *= 2
    kept = sums[0].reshape(n_expert, slots_cap, feat_part)
    given = sums[bit].reshape(n_expert, slots_cap, feat_part)
    returned = {}
    for step in sorted(range(n_expert), key=lambda s: abs(2 * s - n_expert) if s else 2 * n_expert):
        group = lax.rem(my_expert + step, n_expert)
        block = lax.dynamic_index_in_dim(given, group, 0, keepdims=False)
        block = lax.ppermute(block.astype(jnp.bfloat16), "mp", exchange("mp", bit))
        block = lax.dynamic_index_in_dim(kept, group, 0, keepdims=False) + block.astype(jnp.float32)
        block = block.astype(jnp.bfloat16)
        returned[step] = lax.ppermute(block, "expert", shift_by("expert", step)) if step else block
    split = select.reshape(select.shape[0], n_expert, slots_cap)
    chosen = jnp.concatenate(
        [
            lax.dynamic_index_in_dim(split, lax.rem(my_expert - step + n_expert, n_expert), 1, keepdims=False)
            for step in range(n_expert)
        ],
        axis=1,
    )
    grad_tokens = jnp.dot(
        chosen,
        jnp.concatenate([returned[step] for step in range(n_expert)], axis=0).astype(jnp.float32),
        precision=lax.Precision.HIGHEST,
    )
    hidden_out = hidden.reshape(1, 1, n_expert, slots_cap, hidden_part)
    return (hidden_out, grad_tokens.astype(jnp.bfloat16))


def solution(mesh):
    in_specs = (
        P(("dp", "expert"), "mp"),
        P(("dp", "expert"), None),
        P(("dp", "expert"), None),
        P(None, ("dp", "expert"), "mp"),
        P(None, ("dp", "expert"), "mp"),
        P("expert", "dp", None, None, "mp"),
    )
    out_specs = (P("expert", "dp", None, None, "mp"), P(("dp", "expert"), "mp"))
    return jax.shard_map(
        per_device, mesh=mesh, in_specs=in_specs, out_specs=out_specs, check_vma=False
    )
```

time: 589 us -> 386 us (0.66)
  blocking collectives: 198 us -> 0 us
  waiting for transfers between devices: 320 us -> 122 us
  starting transfers between devices: 5.39 us -> 160 us
  Pallas kernels: 0 us -> 46.4 us
  matrix products: 47.1 us -> 1.67 us
  local copies, waits for them, and re-layouts: 2.36 us -> 29.9 us
  other arithmetic: 2.13 us -> 11 us
    all_to_all x4 -> x0, blocking collectives: 198 us -> none  [the longest x1 145 us: per_device(): lax.all_to_all(w_up, 'expert', split_axis=0, concat_axis=1, tiled=True)]
    ppermute x0 -> x46, starting transfers between devices: none -> 160 us  [the longest x15 110 us: to_owner(): piece = lax.ppermute(piece, 'expert', shift_by('expert', step))]
    all_gather x3 -> x1, waiting for transfers between devices: 142 us -> 0.01 us  [per_device(): rows_full = lax.all_gather(slots[:, :feat_part], 'mp', axis=1, tiled=True)]
    all_to_all x1 -> x0, waiting for transfers between devices: 137 us -> none  [per_device(): lax.all_to_all(w_gate, 'expert', split_axis=0, concat_axis=1, tiled=True)]
    ppermute x0 -> x46, waiting for transfers between devices: none -> 122 us  [the longest x15 51 us: to_owner(): piece = lax.ppermute(piece, 'expert', shift_by('expert', step))]
    pallas_call x0 -> x5, Pallas kernels: none -> 46.4 us  [expert_chunk(): pl.pallas_call(functools.partial(expert_kernel, len(parts), carried is No...]
    dot_general x5 -> x1, matrix products: 46.6 us -> 1.22 us  [per_device(): jnp.dot(chosen, jnp.concatenate([returned[step] for step in range(n_exper...]
    reduce_scatter x1 -> x0, waiting for transfers between devices: 40.6 us -> none  [per_device(): lax.psum_scatter(back_term.reshape(n_expert, slots_cap, D), 'mp', scatter...]
  transfers between devices with their start and end apart: 5 -> 47, of which waited for: 3 -> 21; matrix products, arithmetic and copies ran while one was open for 2% -> 6% of each run, Pallas kernels for 0% -> 10%
where the time goes in v1:
time: 386 us
  starting transfers between devices  160 us (41%)
  waiting for transfers between devices  122 us (32%)
  Pallas kernels  46.4 us (12%)
  local copies, waits for them, and re-layouts  29.9 us (8%)
  between operations  14.9 us (4%)
  other arithmetic  11 us (3%)
    ppermute x15, starting transfers between devices, to_owner(): piece = lax.ppermute(piece, 'expert', shift_by('expert', step))  110 us
    ppermute x15, waiting for transfers between devices, to_owner(): piece = lax.ppermute(piece, 'expert', shift_by('expert', step))  51 us
    pallas_call x5, Pallas kernels, expert_chunk(): pl.pallas_call(functools.partial(expert_kernel, len(parts), carried is No...  46.4 us
    ppermute x20, waiting for transfers between devices, to_both(): spread[chunk, step] = lax.ppermute(piece, 'dp', shift_by('dp', 1))  41.3 us
    ppermute x6, starting transfers between devices, per_device(): lax.ppermute(block, 'expert', shift_by('expert', step))  24.4 us
    ppermute x20, starting transfers between devices, to_both(): spread[chunk, step] = lax.ppermute(piece, 'dp', shift_by('dp', 1))  20.9 us
    ppermute x6, waiting for transfers between devices, per_device(): lax.ppermute(block, 'expert', shift_by('expert', step))  17.9 us
    unnamed x109, local copies, waits for them, and re-layouts  15.3 us
  transfers between devices with their start and end apart: 47, of which 21 were waited for; matrix products, arithmetic and copies ran while one was open for 6% of the time, Pallas kernels for 10%

profile of v1, /device:TPU:0, one launch (start us, length us, event | category | flops | bytes accessed | tf_op | source)
XLA Modules:
  0.0 385.5 jit_solution(13374826175231341185)
XLA Ops:
  7.3 3.2 constant_dynamic-slice_fusion.10
  13.5 5.1 %collective-permute-start.2 = (bf16[72,896]{1,0:T(8,128)(2,1)S(1)}, bf16[72,896]{1,0:T(8,128)(2,1)S(1)}, u32[]{:S(2)}, u32[]{:S(2)}) collective-permute-start(bf16[72,896]{1,0:T(8,128)(2,1)S(1)} %get-tuple-element.147), channel_id=1, source_target_pairs={{0,12},{4,0},{8,4},{12,8},{1,13},{5,1},{9,5},{13,9},{2,14},{6,2},{... | collective-permute-start | bytes 387080 | tf_op jit(solution)/shard_map/ppermute | solution.py:212
  19.6 2.8 collective-permute-done.2
  22.5 7.2 %collective-permute-done.1 = bf16[72,896]{1,0:T(8,128)(2,1)S(1)} collective-permute-done((bf16[72,896]{1,0:T(8,128)(2,1)S(1)}, bf16[72,896]{1,0:T(8,128)(2,1)S(1)}, u32[]{:S(2)}, u32[]{:S(2)}) %collective-permute-start.1) | collective-permute-done | bytes 129056 | tf_op jit(solution)/shard_map/ppermute | solution.py:212
  30.8 1.6 collective-permute-start.11
  33.3 2.0 collective-permute-start.13
  35.3 6.0 %constant_dynamic-slice_fusion.8 = (bf16[1,384,512]{2,1,0:T(8,128)(2,1)}, bf16[1,384,512]{2,1,0:T(8,128)(2,1)}, bf16[1,384,512]{2,1,0:T(8,128)(2,1)}, bf16[1,384...) fusion(bf16[4,384,2048]{2,1,0:T(8,128)(2,1)} %param.10, ...), kind=kLoop, calls=%fused_computation.93 | loop fusion | bytes 18874384 | tf_op jit(solution)/shard_map/dynamic_slice | solution.py:145
  41.8 2.9 collective-permute-start.5
  44.7 1.7 collective-permute-done.3.refs_2_
  48.5 13.0 %collective-permute-done.13.refs_4_ = bf16[2,384,256]{2,1,0:T(8,128)(2,1)} collective-permute-done((bf16[2,384,256]{2,1,0:T(8,128)(2,1)S(1)}, bf16[2,384,256]{2,1,0:T(8,128)(2,1)}, u32[]{:S(2)}, u32[]{:S(2)}) %collective-permute-start.13) | collective-permute-done | bytes 393248 | tf_op jit(solution)/shard_map/ppermute | solution.py:163
  61.5 8.4 %collective-permute-start.4 = (bf16[2,384,512]{2,1,0:T(8,128)(2,1)S(1)}, bf16[2,384,512]{2,1,0:T(8,128)(2,1)}, u32[]{:S(2)}, u32[]{:S(2)}) collective-permute-start(bf16[2,384,512]{2,1,0:T(8,128)(2,1)S(1)} %pad_maximum_fusion.1), channel_id=1, source_target_pairs={{0,4},{4,8},{8,12},{12,0},{1,5},{5,9},{9,13},{13,1},{2,6},{6,10},{... | collective-permute-start | bytes 2359304 | tf_op jit(solution)/shard_map/ppermute | solution.py:163
  71.9 3.6 collective-permute-start.17
  75.5 9.1 %collective-permute-done.12.refs_3_ = bf16[2,384,256]{2,1,0:T(8,128)(2,1)S(1)} collective-permute-done((bf16[2,384,256]{2,1,0:T(8,128)(2,1)S(1)}, bf16[2,384,256]{2,1,0:T(8,128)(2,1)S(1)}, u32[]{:S(2)}, u32[]{:S(2)}) %collective-permute-start.12) | collective-permute-done | bytes 393248 | tf_op jit(solution)/shard_map/ppermute | solution.py:175
  84.6 2.6 collective-permute-start.20
  93.1 2.2 pad_maximum_fusion.9
  95.3 2.0 pad_maximum_fusion.10
  97.3 19.0 %collective-permute-done.7.refs_7_ = bf16[2,384,256]{2,1,0:T(8,128)(2,1)} collective-permute-done((bf16[2,384,256]{2,1,0:T(8,128)(2,1)}, bf16[2,384,256]{2,1,0:T(8,128)(2,1)}, u32[]{:S(2)}, u32[]{:S(2)}) %collective-permute-start.7) | collective-permute-done | bytes 393248 | tf_op jit(solution)/shard_map/ppermute | solution.py:175
  116.8 7.9 %collective-permute-done.15.refs_5_ = bf16[2,384,256]{2,1,0:T(8,128)(2,1)} collective-permute-done((bf16[2,384,256]{2,1,0:T(8,128)(2,1)}, bf16[2,384,256]{2,1,0:T(8,128)(2,1)}, u32[]{:S(2)}, u32[]{:S(2)}) %collective-permute-start.15) | collective-permute-done | bytes 393248 | tf_op jit(solution)/shard_map/ppermute | solution.py:175
  124.7 5.1 %collective-permute-start.10 = (bf16[2,384,512]{2,1,0:T(8,128)(2,1)}, bf16[2,384,512]{2,1,0:T(8,128)(2,1)}, u32[]{:S(2)}, u32[]{:S(2)}) collective-permute-start(bf16[2,384,512]{2,1,0:T(8,128)(2,1)} %pad_maximum_fusion.4), channel_id=1, source_target_pairs={{0,4},{4,8},{8,12},{12,0},{1,5},{5,9},{9,13},{13,1},{2,6},{6,10},{... | collective-permute-start | bytes 2359304 | tf_op jit(solution)/shard_map/ppermute | solution.py:163
  130.3 24.4 %collective-permute-start.25 = (bf16[2,384,512]{2,1,0:T(8,128)(2,1)}, bf16[2,384,512]{2,1,0:T(8,128)(2,1)}, u32[]{:S(2)}, u32[]{:S(2)}) collective-permute-start(bf16[2,384,512]{2,1,0:T(8,128)(2,1)} %pad_maximum_fusion.9), channel_id=1, source_target_pairs={{0,8},{4,12},{8,0},{12,4},{1,9},{5,13},{9,1},{13,5},{2,10},{6,14},... | collective-permute-start | bytes 2359304 | tf_op jit(solution)/shard_map/ppermute | solution.py:163
  154.7 3.4 collective-permute-start.27
  166.2 1.6 collective-permute-start.19
  167.8 6.6 %shard_map.77 = (bf16[288,2048]{1,0:T(8,128)(2,1)}, f32[288,3072]{1,0:T(8,128)}, f32[8,128]{1,0:T(8,128)}) custom-call(bf16[288,3072]{1,0:T(8,128)(2,1)} %copy-done.24, f32[288,1]{1,0:T(8,128)S(1)} %maximum_convert_fusion.scale_ref, bf16[288,2048]{1,0:T(8,128)(2,1)S(1)} %bitcast.87, bf16[2,384,256]{2,1,0:T(8,128)(2,1)S(1)} %pad_maximum_fusion.16.refs_0_, ...), custom_call_target="tpu_custom_call" | custom-call | flops 1811939328 | bytes 11993088 | tf_op jit(solution)/shard_map/pallas_call | solution.py:104
  176.0 14.3 %collective-permute-done.25.refs_4_ = bf16[2,384,512]{2,1,0:T(8,128)(2,1)} collective-permute-done((bf16[2,384,512]{2,1,0:T(8,128)(2,1)}, bf16[2,384,512]{2,1,0:T(8,128)(2,1)}, u32[]{:S(2)}, u32[]{:S(2)}) %collective-permute-start.25) | collective-permute-done | bytes 786464 | tf_op jit(solution)/shard_map/ppermute | solution.py:163
  191.8 3.6 collective-permute-done.9.refs_1_
  196.9 26.0 %collective-permute-start.30 = (bf16[2,384,512]{2,1,0:T(8,128)(2,1)S(1)}, bf16[2,384,512]{2,1,0:T(8,128)(2,1)S(1)}, u32[]{:S(2)}, u32[]{:S(2)}) collective-permute-start(bf16[2,384,512]{2,1,0:T(8,128)(2,1)S(1)} %pad_maximum_fusion.11), channel_id=1, source_target_pairs={{0,8},{4,12},{8,0},{12,4},{1,9},{5,13},{9,1},{13,5},{2,10},{6,14},... | collective-permute-start | bytes 2359304 | tf_op jit(solution)/shard_map/ppermute | solution.py:163
  224.4 3.4 collective-permute-start.34
  227.9 11.0 %shard_map.78 = (bf16[288,2048]{1,0:T(8,128)(2,1)}, f32[288,3072]{1,0:T(8,128)}, f32[8,128]{1,0:T(8,128)}) custom-call(bf16[288,3072]{1,0:T(8,128)(2,1)} %copy-done.24, f32[288,1]{1,0:T(8,128)S(1)} %maximum_convert_fusion.scale_ref, bf16[288,2048]{1,0:T(8,128)(2,1)} %bitcast.84, ...), custom_call_target="tpu_custom_call", output_to_operand_aliasing={{1}: (11, {}), {0}: (12, {})} | custom-call | flops 3623878656 | bytes 15138816 | tf_op jit(solution)/shard_map/pallas_call | solution.py:104
  239.5 5.1 %collective-permute-start.22 = (bf16[2,384,256]{2,1,0:T(8,128)(2,1)S(1)}, bf16[2,384,256]{2,1,0:T(8,128)(2,1)}, u32[]{:S(2)}, u32[]{:S(2)}) collective-permute-start(bf16[2,384,256]{2,1,0:T(8,128)(2,1)S(1)} %pad_maximum_fusion.20), channel_id=1, source_target_pairs={{0,4},{4,8},{8,12},{12,0},{1,5},{5,9},{9,13},{13,1},{2,6},{6,10},{... | collective-permute-start | bytes 1179656 | tf_op jit(solution)/shard_map/ppermute | solution.py:163
  244.6 17.8 %collective-permute-done.30.refs_4_ = bf16[2,384,512]{2,1,0:T(8,128)(2,1)S(1)} collective-permute-done((bf16[2,384,512]{2,1,0:T(8,128)(2,1)S(1)}, bf16[2,384,512]{2,1,0:T(8,128)(2,1)S(1)}, u32[]{:S(2)}, u32[]{:S(2)}) %collective-permute-start.30) | collective-permute-done | bytes 786464 | tf_op jit(solution)/shard_map/ppermute | solution.py:163
  264.6 19.1 %collective-permute-start.31 = (bf16[2,384,256]{2,1,0:T(8,128)(2,1)S(1)}, bf16[2,384,256]{2,1,0:T(8,128)(2,1)}, u32[]{:S(2)}, u32[]{:S(2)}) collective-permute-start(bf16[2,384,256]{2,1,0:T(8,128)(2,1)S(1)} %pad_maximum_fusion.22), channel_id=1, source_target_pairs={{0,8},{4,12},{8,0},{12,4},{1,9},{5,13},{9,1},{13,5},{2,10},{6,14},... | collective-permute-start | bytes 1179656 | tf_op jit(solution)/shard_map/ppermute | solution.py:163
  283.7 3.4 collective-permute-start.35
  287.2 10.7 %shard_map.79 = (bf16[288,2048]{1,0:T(8,128)(2,1)}, f32[288,3072]{1,0:T(8,128)}, f32[8,128]{1,0:T(8,128)}) custom-call(bf16[288,3072]{1,0:T(8,128)(2,1)} %copy-done.24, f32[288,1]{1,0:T(8,128)S(1)} %maximum_convert_fusion.scale_ref, bf16[288,2048]{1,0:T(8,128)(2,1)} %bitcast.85, ...), custom_call_target="tpu_custom_call", output_to_operand_aliasing={{1}: (11, {}), {0}: (12, {})} | custom-call | flops 3623878656 | bytes 15138816 | tf_op jit(solution)/shard_map/pallas_call | solution.py:104
  298.9 3.4 collective-permute-done.31.refs_4_
  304.1 3.7 collective-permute-start.37
  312.4 10.5 %shard_map.80 = (bf16[288,2048]{1,0:T(8,128)(2,1)}, f32[288,3072]{1,0:T(8,128)}, f32[8,128]{1,0:T(8,128)}) custom-call(bf16[288,3072]{1,0:T(8,128)(2,1)} %copy-done.24, f32[288,1]{1,0:T(8,128)S(1)} %maximum_convert_fusion.scale_ref, bf16[288,2048]{1,0:T(8,128)(2,1)} %bitcast.86, ...), custom_call_target="tpu_custom_call", output_to_operand_aliasing={{1}: (11, {}), {0}: (12, {})} | custom-call | flops 3623878656 | bytes 15138816 | tf_op jit(solution)/shard_map/pallas_call | solution.py:104
  322.9 1.8 collective-permute-done.37.refs_7_
  324.7 7.6 %shard_map.81 = (bf16[288,2048]{1,0:T(8,128)(2,1)}, f32[288,3072]{1,0:T(8,128)}, f32[8,128]{1,0:T(8,128)}) custom-call(bf16[288,3072]{1,0:T(8,128)(2,1)} %copy-done.24, f32[288,1]{1,0:T(8,128)S(1)} %maximum_convert_fusion.scale_ref, bf16[288,2048]{1,0:T(8,128)(2,1)S(1)} %bitcast.88, ...), custom_call_target="tpu_custom_call", output_to_operand_aliasing={{1}: (11, {}), {0}: (12, {})} | custom-call | flops 1811939328 | bytes 11993088 | tf_op jit(solution)/shard_map/pallas_call | solution.py:104
  332.3 2.2 constant_dynamic-slice_fusion.7
  334.8 3.7 collective-permute-done.38
  338.8 1.6 collective-permute-start.39
  343.0 1.8 collective-permute-done.39
  344.8 2.4 collective-permute-done.44
  347.1 2.4 collective-permute-done.42
  349.5 1.6 collective-permute-done.40
  351.2 17.4 %collective-permute-start.45 = (bf16[72,768]{1,0:T(8,128)(2,1)S(1)}, bf16[72,768]{1,0:T(8,128)(2,1)S(1)}, u32[]{:S(2)}, u32[]{:S(2)}) collective-permute-start(bf16[72,768]{1,0:T(8,128)(2,1)S(1)} %get-tuple-element.139), channel_id=1, source_target_pairs={{0,12},{4,0},{8,4},{12,8},{1,13},{5,1},{9,5},{13,9},{2,14},{6,2},{... | collective-permute-start | bytes 331784 | tf_op jit(solution)/shard_map/ppermute | solution.py:275
  369.5 2.6 collective-permute-done.45
  372.2 5.3 %collective-permute-done.43 = bf16[72,768]{1,0:T(8,128)(2,1)S(1)} collective-permute-done((bf16[72,768]{1,0:T(8,128)(2,1)S(1)}, bf16[72,768]{1,0:T(8,128)(2,1)S(1)}, u32[]{:S(2)}, u32[]{:S(2)}) %collective-permute-start.43) | collective-permute-done | bytes 110624 | tf_op jit(solution)/shard_map/ppermute | solution.py:275
  (221 shorter events, 47.2 us)
Async XLA Ops:
  7.2 150.9 %all-gather.2.cloned.1.call-start = ((), (), s32[]{:S(2)}) async-start(), calls=%async_computation | async-start | bytes 2211840 | tf_op jit(solution)/shard_map/all_gather | solution.py:222
  13.5 9.0 %collective-permute-start.2 = (bf16[72,896]{1,0:T(8,128)(2,1)S(1)}, bf16[72,896]{1,0:T(8,128)(2,1)S(1)}, u32[]{:S(2)}, u32[]{:S(2)}) collective-permute-start(bf16[72,896]{1,0:T(8,128)(2,1)S(1)} %get-tuple-element.147), channel_id=1, source_target_pairs={{0,12},{4,0},{8,4},{12,8},{1,13},{5,1},{9,5},{13,9},{2,14},{6,2},{... | collective-permute-start | bytes 387080 | tf_op jit(solution)/shard_map/ppermute | solution.py:212
  18.6 11.0 %collective-permute-start.1 = (bf16[72,896]{1,0:T(8,128)(2,1)S(1)}, bf16[72,896]{1,0:T(8,128)(2,1)S(1)}, u32[]{:S(2)}, u32[]{:S(2)}) collective-permute-start(bf16[72,896]{1,0:T(8,128)(2,1)S(1)} %get-tuple-element.148), channel_id=1, source_target_pairs={{0,8},{4,12},{8,0},{12,4},{1,9},{5,13},{9,1},{13,5},{2,10},{6,14},... | collective-permute-start | bytes 387080 | tf_op jit(solution)/shard_map/ppermute | solution.py:212
  18.6 11.0 %collective-permute-start = (bf16[72,896]{1,0:T(8,128)(2,1)S(1)}, bf16[72,896]{1,0:T(8,128)(2,1)S(1)}, u32[]{:S(2)}, u32[]{:S(2)}) collective-permute-start(bf16[72,896]{1,0:T(8,128)(2,1)S(1)} %get-tuple-element.149), channel_id=1, source_target_pairs={{0,4},{4,8},{8,12},{12,0},{1,5},{5,9},{9,13},{13,1},{2,6},{6,10},{... | collective-permute-start | bytes 387080 | tf_op jit(solution)/shard_map/ppermute | solution.py:212
  30.8 16.1 %collective-permute-start.11 = (bf16[2,384,256]{2,1,0:T(8,128)(2,1)S(1)}, bf16[2,384,256]{2,1,0:T(8,128)(2,1)S(1)}, u32[]{:S(2)}, u32[]{:S(2)}) collective-permute-start(bf16[2,384,256]{2,1,0:T(8,128)(2,1)S(1)} %pad_maximum_fusion.16.refs_0_), channel_id=1, source_target_pairs={{0,16},{16,0},{1,17},{17,1},{2,18},{18,2},{3,19},{19,3},{4,20},{20... | collective-permute-start | bytes 1179656 | tf_op jit(solution)/shard_map/ppermute | solution.py:175
  32.4 14.0 %collective-permute-start.3 = (bf16[2,384,256]{2,1,0:T(8,128)(2,1)S(1)}, bf16[2,384,256]{2,1,0:T(8,128)(2,1)S(1)}, u32[]{:S(2)}, u32[]{:S(2)}) collective-permute-start(bf16[2,384,256]{2,1,0:T(8,128)(2,1)S(1)} %pad_maximum_fusion.18), channel_id=1, source_target_pairs={{0,4},{4,8},{8,12},{12,0},{1,5},{5,9},{9,13},{13,1},{2,6},{6,10},{... | collective-permute-start | bytes 1179656 | tf_op jit(solution)/shard_map/ppermute | solution.py:163
  33.3 28.3 %collective-permute-start.13 = (bf16[2,384,256]{2,1,0:T(8,128)(2,1)S(1)}, bf16[2,384,256]{2,1,0:T(8,128)(2,1)}, u32[]{:S(2)}, u32[]{:S(2)}) collective-permute-start(bf16[2,384,256]{2,1,0:T(8,128)(2,1)S(1)} %pad_maximum_fusion.21), channel_id=1, source_target_pairs={{0,8},{4,12},{8,0},{12,4},{1,9},{5,13},{9,1},{13,5},{2,10},{6,14},... | collective-permute-start | bytes 1179656 | tf_op jit(solution)/shard_map/ppermute | solution.py:163
  41.4 45.8 %collective-permute-start.6 = (bf16[2,384,512]{2,1,0:T(8,128)(2,1)S(1)}, bf16[2,384,512]{2,1,0:T(8,128)(2,1)S(1)}, u32[]{:S(2)}, u32[]{:S(2)}) collective-permute-start(bf16[2,384,512]{2,1,0:T(8,128)(2,1)S(1)} %pad_maximum_fusion.2.refs_0_), channel_id=1, source_target_pairs={{0,16},{16,0},{1,17},{17,1},{2,18},{18,2},{3,19},{19,3},{4,20},{20... | collective-permute-start | bytes 2359304 | tf_op jit(solution)/shard_map/ppermute | solution.py:175
  41.8 30.1 %collective-permute-start.5 = (bf16[2,384,256]{2,1,0:T(8,128)(2,1)S(1)}, bf16[2,384,256]{2,1,0:T(8,128)(2,1)}, u32[]{:S(2)}, u32[]{:S(2)}) collective-permute-start(bf16[2,384,256]{2,1,0:T(8,128)(2,1)S(1)} %pad_maximum_fusion.19), channel_id=1, source_target_pairs={{0,12},{4,0},{8,4},{12,8},{1,13},{5,1},{9,5},{13,9},{2,14},{6,2},{... | collective-permute-start | bytes 1179656 | tf_op jit(solution)/shard_map/ppermute | solution.py:163
  46.4 42.4 %collective-permute-start.14 = (bf16[2,384,512]{2,1,0:T(8,128)(2,1)S(1)}, bf16[2,384,512]{2,1,0:T(8,128)(2,1)S(1)}, u32[]{:S(2)}, u32[]{:S(2)}) collective-permute-start(bf16[2,384,512]{2,1,0:T(8,128)(2,1)S(1)} %pad_maximum_fusion.5.refs_0_), channel_id=1, source_target_pairs={{0,16},{16,0},{1,17},{17,1},{2,18},{18,2},{3,19},{19,3},{4,20},{20... | collective-permute-start | bytes 2359304 | tf_op jit(solution)/shard_map/ppermute | solution.py:175
  46.9 37.6 %collective-permute-start.12 = (bf16[2,384,256]{2,1,0:T(8,128)(2,1)S(1)}, bf16[2,384,256]{2,1,0:T(8,128)(2,1)S(1)}, u32[]{:S(2)}, u32[]{:S(2)}) collective-permute-start(bf16[2,384,256]{2,1,0:T(8,128)(2,1)S(1)} %collective-permute-done.3.refs_2_), channel_id=1, source_target_pairs={{0,16},{16,0},{1,17},{17,1},{2,18},{18,2},{3,19},{19,3},{4,20},{20... | collective-permute-start | bytes 1179656 | tf_op jit(solution)/shard_map/ppermute | solution.py:175
  61.5 30.0 %collective-permute-start.4 = (bf16[2,384,512]{2,1,0:T(8,128)(2,1)S(1)}, bf16[2,384,512]{2,1,0:T(8,128)(2,1)}, u32[]{:S(2)}, u32[]{:S(2)}) collective-permute-start(bf16[2,384,512]{2,1,0:T(8,128)(2,1)S(1)} %pad_maximum_fusion.1), channel_id=1, source_target_pairs={{0,4},{4,8},{8,12},{12,0},{1,5},{5,9},{9,13},{13,1},{2,6},{6,10},{... | collective-permute-start | bytes 2359304 | tf_op jit(solution)/shard_map/ppermute | solution.py:163
  71.9 58.4 %collective-permute-start.17 = (bf16[2,384,512]{2,1,0:T(8,128)(2,1)}, bf16[2,384,512]{2,1,0:T(8,128)(2,1)}, u32[]{:S(2)}, u32[]{:S(2)}) collective-permute-start(bf16[2,384,512]{2,1,0:T(8,128)(2,1)} %pad_maximum_fusion.6), channel_id=1, source_target_pairs={{0,8},{4,12},{8,0},{12,4},{1,9},{5,13},{9,1},{13,5},{2,10},{6,14},... | collective-permute-start | bytes 2359304 | tf_op jit(solution)/shard_map/ppermute | solution.py:163
  84.6 45.7 %collective-permute-start.20 = (bf16[2,384,512]{2,1,0:T(8,128)(2,1)}, bf16[2,384,512]{2,1,0:T(8,128)(2,1)}, u32[]{:S(2)}, u32[]{:S(2)}) collective-permute-start(bf16[2,384,512]{2,1,0:T(8,128)(2,1)} %pad_maximum_fusion.8), channel_id=1, source_target_pairs={{0,12},{4,0},{8,4},{12,8},{1,13},{5,1},{9,5},{13,9},{2,14},{6,2},{... | collective-permute-start | bytes 2359304 | tf_op jit(solution)/shard_map/ppermute | solution.py:163
  87.2 67.5 %collective-permute-start.18 = (bf16[2,384,512]{2,1,0:T(8,128)(2,1)S(1)}, bf16[2,384,512]{2,1,0:T(8,128)(2,1)}, u32[]{:S(2)}, u32[]{:S(2)}) collective-permute-start(bf16[2,384,512]{2,1,0:T(8,128)(2,1)S(1)} %pad_maximum_fusion.7.refs_0_), channel_id=1, source_target_pairs={{0,16},{16,0},{1,17},{17,1},{2,18},{18,2},{3,19},{19,3},{4,20},{20... | collective-permute-start | bytes 2359304 | tf_op jit(solution)/shard_map/ppermute | solution.py:175
  89.7 26.6 %collective-permute-start.7 = (bf16[2,384,256]{2,1,0:T(8,128)(2,1)}, bf16[2,384,256]{2,1,0:T(8,128)(2,1)}, u32[]{:S(2)}, u32[]{:S(2)}) collective-permute-start(bf16[2,384,256]{2,1,0:T(8,128)(2,1)} %collective-permute-done.5.refs_6_), channel_id=1, source_target_pairs={{0,16},{16,0},{1,17},{17,1},{2,18},{18,2},{3,19},{19,3},{4,20},{20... | collective-permute-start | bytes 1179656 | tf_op jit(solution)/shard_map/ppermute | solution.py:175
  91.5 33.2 %collective-permute-start.15 = (bf16[2,384,256]{2,1,0:T(8,128)(2,1)}, bf16[2,384,256]{2,1,0:T(8,128)(2,1)}, u32[]{:S(2)}, u32[]{:S(2)}) collective-permute-start(bf16[2,384,256]{2,1,0:T(8,128)(2,1)} %collective-permute-done.13.refs_4_), channel_id=1, source_target_pairs={{0,16},{16,0},{1,17},{17,1},{2,18},{18,2},{3,19},{19,3},{4,20},{20... | collective-permute-start | bytes 1179656 | tf_op jit(solution)/shard_map/ppermute | solution.py:175
  97.3 70.4 %copy-start.2 = (bf16[1,1,4,72,2048]{4,3,2,1,0:T(8,128)(2,1)S(1)}, bf16[1,1,4,72,2048]{4,3,2,1,0:T(8,128)(2,1)}, u32[]{:S(2)}) copy-start(bf16[1,1,4,72,2048]{4,3,2,1,0:T(8,128)(2,1)} %param.11) | copy-start | bytes 3538948
  116.3 58.1 %collective-permute-start.8 = (bf16[2,384,512]{2,1,0:T(8,128)(2,1)}, bf16[2,384,512]{2,1,0:T(8,128)(2,1)}, u32[]{:S(2)}, u32[]{:S(2)}) collective-permute-start(bf16[2,384,512]{2,1,0:T(8,128)(2,1)} %collective-permute-done.4.refs_2_), channel_id=1, source_target_pairs={{0,16},{16,0},{1,17},{17,1},{2,18},{18,2},{3,19},{19,3},{4,20},{20... | collective-permute-start | bytes 2359304 | tf_op jit(solution)/shard_map/ppermute | solution.py:175
  124.7 41.4 %collective-permute-start.10 = (bf16[2,384,512]{2,1,0:T(8,128)(2,1)}, bf16[2,384,512]{2,1,0:T(8,128)(2,1)}, u32[]{:S(2)}, u32[]{:S(2)}) collective-permute-start(bf16[2,384,512]{2,1,0:T(8,128)(2,1)} %pad_maximum_fusion.4), channel_id=1, source_target_pairs={{0,4},{4,8},{8,12},{12,0},{1,5},{5,9},{9,13},{13,1},{2,6},{6,10},{... | collective-permute-start | bytes 2359304 | tf_op jit(solution)/shard_map/ppermute | solution.py:163
  130.3 44.3 %collective-permute-start.21 = (bf16[2,384,512]{2,1,0:T(8,128)(2,1)}, bf16[2,384,512]{2,1,0:T(8,128)(2,1)}, u32[]{:S(2)}, u32[]{:S(2)}) collective-permute-start(bf16[2,384,512]{2,1,0:T(8,128)(2,1)} %collective-permute-done.20.refs_6_), channel_id=1, source_target_pairs={{0,16},{16,0},{1,17},{17,1},{2,18},{18,2},{3,19},{19,3},{4,20},{20... | collective-permute-start | bytes 2359304 | tf_op jit(solution)/shard_map/ppermute | solution.py:175
  130.3 60.0 %collective-permute-start.25 = (bf16[2,384,512]{2,1,0:T(8,128)(2,1)}, bf16[2,384,512]{2,1,0:T(8,128)(2,1)}, u32[]{:S(2)}, u32[]{:S(2)}) collective-permute-start(bf16[2,384,512]{2,1,0:T(8,128)(2,1)} %pad_maximum_fusion.9), channel_id=1, source_target_pairs={{0,8},{4,12},{8,0},{12,4},{1,9},{5,13},{9,1},{13,5},{2,10},{6,14},... | collective-permute-start | bytes 2359304 | tf_op jit(solution)/shard_map/ppermute | solution.py:163
  154.7 42.1 %collective-permute-start.27 = (bf16[2,384,512]{2,1,0:T(8,128)(2,1)}, bf16[2,384,512]{2,1,0:T(8,128)(2,1)}, u32[]{:S(2)}, u32[]{:S(2)}) collective-permute-start(bf16[2,384,512]{2,1,0:T(8,128)(2,1)} %pad_maximum_fusion.10), channel_id=1, source_target_pairs={{0,12},{4,0},{8,4},{12,8},{1,13},{5,1},{9,5},{13,9},{2,14},{6,2},{... | collective-permute-start | bytes 2359304 | tf_op jit(solution)/shard_map/ppermute | solution.py:163
  166.2 30.7 %collective-permute-start.19 = (bf16[2,384,512]{2,1,0:T(8,128)(2,1)}, bf16[2,384,512]{2,1,0:T(8,128)(2,1)S(1)}, u32[]{:S(2)}, u32[]{:S(2)}) collective-permute-start(bf16[2,384,512]{2,1,0:T(8,128)(2,1)} %collective-permute-done.17.refs_4_), channel_id=1, source_target_pairs={{0,16},{16,0},{1,17},{17,1},{2,18},{18,2},{3,19},{19,3},{4,20},{20... | collective-permute-start | bytes 2359304 | tf_op jit(solution)/shard_map/ppermute | solution.py:175
  174.4 50.0 %collective-permute-start.16 = (bf16[2,384,512]{2,1,0:T(8,128)(2,1)S(1)}, bf16[2,384,512]{2,1,0:T(8,128)(2,1)S(1)}, u32[]{:S(2)}, u32[]{:S(2)}) collective-permute-start(bf16[2,384,512]{2,1,0:T(8,128)(2,1)S(1)} %copy-done.46), channel_id=1, source_target_pairs={{0,4},{4,8},{8,12},{12,0},{1,5},{5,9},{9,13},{13,1},{2,6},{6,10},{... | collective-permute-start | bytes 2359304 | tf_op jit(solution)/shard_map/ppermute | solution.py:163
  174.6 20.8 %collective-permute-start.9 = (bf16[2,384,256]{2,1,0:T(8,128)(2,1)S(1)}, bf16[2,384,256]{2,1,0:T(8,128)(2,1)S(1)}, u32[]{:S(2)}, u32[]{:S(2)}) collective-permute-start(bf16[2,384,256]{2,1,0:T(8,128)(2,1)S(1)} %pad_maximum_fusion.17.refs_0_), channel_id=1, source_target_pairs={{0,16},{16,0},{1,17},{17,1},{2,18},{18,2},{3,19},{19,3},{4,20},{20... | collective-permute-start | bytes 1179656 | tf_op jit(solution)/shard_map/ppermute | solution.py:175
  190.3 48.6 %collective-permute-start.23 = (bf16[2,384,512]{2,1,0:T(8,128)(2,1)}, bf16[2,384,512]{2,1,0:T(8,128)(2,1)S(1)}, u32[]{:S(2)}, u32[]{:S(2)}) collective-permute-start(bf16[2,384,512]{2,1,0:T(8,128)(2,1)} %collective-permute-done.10.refs_2_), channel_id=1, source_target_pairs={{0,16},{16,0},{1,17},{17,1},{2,18},{18,2},{3,19},{19,3},{4,20},{20... | collective-permute-start | bytes 2359304 | tf_op jit(solution)/shard_map/ppermute | solution.py:175
  195.4 44.1 %collective-permute-start.26 = (bf16[2,384,512]{2,1,0:T(8,128)(2,1)}, bf16[2,384,512]{2,1,0:T(8,128)(2,1)S(1)}, u32[]{:S(2)}, u32[]{:S(2)}) collective-permute-start(bf16[2,384,512]{2,1,0:T(8,128)(2,1)} %collective-permute-done.25.refs_4_), channel_id=1, source_target_pairs={{0,16},{16,0},{1,17},{17,1},{2,18},{18,2},{3,19},{19,3},{4,20},{20... | collective-permute-start | bytes 2359304 | tf_op jit(solution)/shard_map/ppermute | solution.py:175
  196.9 65.5 %collective-permute-start.30 = (bf16[2,384,512]{2,1,0:T(8,128)(2,1)S(1)}, bf16[2,384,512]{2,1,0:T(8,128)(2,1)S(1)}, u32[]{:S(2)}, u32[]{:S(2)}) collective-permute-start(bf16[2,384,512]{2,1,0:T(8,128)(2,1)S(1)} %pad_maximum_fusion.11), channel_id=1, source_target_pairs={{0,8},{4,12},{8,0},{12,4},{1,9},{5,13},{9,1},{13,5},{2,10},{6,14},... | collective-permute-start | bytes 2359304 | tf_op jit(solution)/shard_map/ppermute | solution.py:163
  222.9 41.0 %collective-permute-start.28 = (bf16[2,384,512]{2,1,0:T(8,128)(2,1)}, bf16[2,384,512]{2,1,0:T(8,128)(2,1)S(1)}, u32[]{:S(2)}, u32[]{:S(2)}) collective-permute-start(bf16[2,384,512]{2,1,0:T(8,128)(2,1)} %collective-permute-done.27.refs_6_), channel_id=1, source_target_pairs={{0,16},{16,0},{1,17},{17,1},{2,18},{18,2},{3,19},{19,3},{4,20},{20... | collective-permute-start | bytes 2359304 | tf_op jit(solution)/shard_map/ppermute | solution.py:175
  224.4 39.5 %collective-permute-start.34 = (bf16[2,384,512]{2,1,0:T(8,128)(2,1)S(1)}, bf16[2,384,512]{2,1,0:T(8,128)(2,1)S(1)}, u32[]{:S(2)}, u32[]{:S(2)}) collective-permute-start(bf16[2,384,512]{2,1,0:T(8,128)(2,1)S(1)} %pad_maximum_fusion.12), channel_id=1, source_target_pairs={{0,12},{4,0},{8,4},{12,8},{1,13},{5,1},{9,5},{13,9},{2,14},{6,2},{... | collective-permute-start | bytes 2359304 | tf_op jit(solution)/shard_map/ppermute | solution.py:163
  238.9 59.0 %collective-permute-start.24 = (bf16[2,384,512]{2,1,0:T(8,128)(2,1)S(1)}, bf16[2,384,512]{2,1,0:T(8,128)(2,1)S(1)}, u32[]{:S(2)}, u32[]{:S(2)}) collective-permute-start(bf16[2,384,512]{2,1,0:T(8,128)(2,1)S(1)} %collective-permute-done.16.refs_2_), channel_id=1, source_target_pairs={{0,16},{16,0},{1,17},{17,1},{2,18},{18,2},{3,19},{19,3},{4,20},{20... | collective-permute-start | bytes 2359304 | tf_op jit(solution)/shard_map/ppermute | solution.py:175
  239.5 44.2 %collective-permute-start.22 = (bf16[2,384,256]{2,1,0:T(8,128)(2,1)S(1)}, bf16[2,384,256]{2,1,0:T(8,128)(2,1)}, u32[]{:S(2)}, u32[]{:S(2)}) collective-permute-start(bf16[2,384,256]{2,1,0:T(8,128)(2,1)S(1)} %pad_maximum_fusion.20), channel_id=1, source_target_pairs={{0,4},{4,8},{8,12},{12,0},{1,5},{5,9},{9,13},{13,1},{2,6},{6,10},{... | collective-permute-start | bytes 1179656 | tf_op jit(solution)/shard_map/ppermute | solution.py:163
  262.4 39.9 %collective-permute-start.32 = (bf16[2,384,512]{2,1,0:T(8,128)(2,1)S(1)}, bf16[2,384,512]{2,1,0:T(8,128)(2,1)S(1)}, u32[]{:S(2)}, u32[]{:S(2)}) collective-permute-start(bf16[2,384,512]{2,1,0:T(8,128)(2,1)S(1)} %collective-permute-done.30.refs_4_), channel_id=1, source_target_pairs={{0,16},{16,0},{1,17},{17,1},{2,18},{18,2},{3,19},{19,3},{4,20},{20... | collective-permute-start | bytes 2359304 | tf_op jit(solution)/shard_map/ppermute | solution.py:175
  263.9 39.3 %collective-permute-start.36 = (bf16[2,384,512]{2,1,0:T(8,128)(2,1)S(1)}, bf16[2,384,512]{2,1,0:T(8,128)(2,1)S(1)}, u32[]{:S(2)}, u32[]{:S(2)}) collective-permute-start(bf16[2,384,512]{2,1,0:T(8,128)(2,1)S(1)} %collective-permute-done.34.refs_6_), channel_id=1, source_target_pairs={{0,16},{16,0},{1,17},{17,1},{2,18},{18,2},{3,19},{19,3},{4,20},{20... | collective-permute-start | bytes 2359304 | tf_op jit(solution)/shard_map/ppermute | solution.py:175
  264.6 37.7 %collective-permute-start.31 = (bf16[2,384,256]{2,1,0:T(8,128)(2,1)S(1)}, bf16[2,384,256]{2,1,0:T(8,128)(2,1)}, u32[]{:S(2)}, u32[]{:S(2)}) collective-permute-start(bf16[2,384,256]{2,1,0:T(8,128)(2,1)S(1)} %pad_maximum_fusion.22), channel_id=1, source_target_pairs={{0,8},{4,12},{8,0},{12,4},{1,9},{5,13},{9,1},{13,5},{2,10},{6,14},... | collective-permute-start | bytes 1179656 | tf_op jit(solution)/shard_map/ppermute | solution.py:163
  283.7 19.4 %collective-permute-start.35 = (bf16[2,384,256]{2,1,0:T(8,128)(2,1)S(1)}, bf16[2,384,256]{2,1,0:T(8,128)(2,1)}, u32[]{:S(2)}, u32[]{:S(2)}) collective-permute-start(bf16[2,384,256]{2,1,0:T(8,128)(2,1)S(1)} %pad_maximum_fusion.23), channel_id=1, source_target_pairs={{0,12},{4,0},{8,4},{12,8},{1,13},{5,1},{9,5},{13,9},{2,14},{6,2},{... | collective-permute-start | bytes 1179656 | tf_op jit(solution)/shard_map/ppermute | solution.py:163
  298.8 24.1 %collective-permute-start.29 = (bf16[2,384,256]{2,1,0:T(8,128)(2,1)}, bf16[2,384,256]{2,1,0:T(8,128)(2,1)S(1)}, u32[]{:S(2)}, u32[]{:S(2)}) collective-permute-start(bf16[2,384,256]{2,1,0:T(8,128)(2,1)} %collective-permute-done.22.refs_2_), channel_id=1, source_target_pairs={{0,16},{16,0},{1,17},{17,1},{2,18},{18,2},{3,19},{19,3},{4,20},{20... | collective-permute-start | bytes 1179656 | tf_op jit(solution)/shard_map/ppermute | solution.py:175
  303.2 19.8 %collective-permute-start.33 = (bf16[2,384,256]{2,1,0:T(8,128)(2,1)}, bf16[2,384,256]{2,1,0:T(8,128)(2,1)S(1)}, u32[]{:S(2)}, u32[]{:S(2)}) collective-permute-start(bf16[2,384,256]{2,1,0:T(8,128)(2,1)} %collective-permute-done.31.refs_4_), channel_id=1, source_target_pairs={{0,16},{16,0},{1,17},{17,1},{2,18},{18,2},{3,19},{19,3},{4,20},{20... | collective-permute-start | bytes 1179656 | tf_op jit(solution)/shard_map/ppermute | solution.py:175
  304.1 20.6 %collective-permute-start.37 = (bf16[2,384,256]{2,1,0:T(8,128)(2,1)}, bf16[2,384,256]{2,1,0:T(8,128)(2,1)}, u32[]{:S(2)}, u32[]{:S(2)}) collective-permute-start(bf16[2,384,256]{2,1,0:T(8,128)(2,1)} %collective-permute-done.35.refs_6_), channel_id=1, source_target_pairs={{0,16},{16,0},{1,17},{17,1},{2,18},{18,2},{3,19},{19,3},{4,20},{20... | collective-permute-start | bytes 1179656 | tf_op jit(solution)/shard_map/ppermute | solution.py:175
  334.8 3.8 collective-permute-start.38
  338.8 6.0 %collective-permute-start.39 = (bf16[72,768]{1,0:T(8,128)(2,1)S(1)}, bf16[72,768]{1,0:T(8,128)(2,1)S(1)}, u32[]{:S(2)}, u32[]{:S(2)}) collective-permute-start(bf16[72,768]{1,0:T(8,128)(2,1)S(1)} %get-tuple-element.150), channel_id=1, source_target_pairs={{0,2},{1,3},{2,0},{3,1},{4,6},{5,7},{6,4},{7,5},{8,10},{9,11},{10,... | collective-permute-start | bytes 331784 | tf_op jit(solution)/shard_map/ppermute | solution.py:272
  340.4 6.7 %collective-permute-start.44 = (bf16[72,768]{1,0:T(8,128)(2,1)S(1)}, bf16[72,768]{1,0:T(8,128)(2,1)S(1)}, u32[]{:S(2)}, u32[]{:S(2)}) collective-permute-start(bf16[72,768]{1,0:T(8,128)(2,1)S(1)} %get-tuple-element.151), channel_id=1, source_target_pairs={{0,2},{1,3},{2,0},{3,1},{4,6},{5,7},{6,4},{7,5},{8,10},{9,11},{10,... | collective-permute-start | bytes 331784 | tf_op jit(solution)/shard_map/ppermute | solution.py:272
  340.9 8.6 %collective-permute-start.42 = (bf16[72,768]{1,0:T(8,128)(2,1)S(1)}, bf16[72,768]{1,0:T(8,128)(2,1)S(1)}, u32[]{:S(2)}, u32[]{:S(2)}) collective-permute-start(bf16[72,768]{1,0:T(8,128)(2,1)S(1)} %get-tuple-element.152), channel_id=1, source_target_pairs={{0,2},{1,3},{2,0},{3,1},{4,6},{5,7},{6,4},{7,5},{8,10},{9,11},{10,... | collective-permute-start | bytes 331784 | tf_op jit(solution)/shard_map/ppermute | solution.py:272
  342.4 8.6 %collective-permute-start.40 = (bf16[72,768]{1,0:T(8,128)(2,1)S(1)}, bf16[72,768]{1,0:T(8,128)(2,1)S(1)}, u32[]{:S(2)}, u32[]{:S(2)}) collective-permute-start(bf16[72,768]{1,0:T(8,128)(2,1)S(1)} %get-tuple-element.153), channel_id=1, source_target_pairs={{0,2},{1,3},{2,0},{3,1},{4,6},{5,7},{6,4},{7,5},{8,10},{9,11},{10,... | collective-permute-start | bytes 331784 | tf_op jit(solution)/shard_map/ppermute | solution.py:272
  351.2 21.0 %collective-permute-start.45 = (bf16[72,768]{1,0:T(8,128)(2,1)S(1)}, bf16[72,768]{1,0:T(8,128)(2,1)S(1)}, u32[]{:S(2)}, u32[]{:S(2)}) collective-permute-start(bf16[72,768]{1,0:T(8,128)(2,1)S(1)} %get-tuple-element.139), channel_id=1, source_target_pairs={{0,12},{4,0},{8,4},{12,8},{1,13},{5,1},{9,5},{13,9},{2,14},{6,2},{... | collective-permute-start | bytes 331784 | tf_op jit(solution)/shard_map/ppermute | solution.py:275
  368.7 8.8 %collective-permute-start.43 = (bf16[72,768]{1,0:T(8,128)(2,1)S(1)}, bf16[72,768]{1,0:T(8,128)(2,1)S(1)}, u32[]{:S(2)}, u32[]{:S(2)}) collective-permute-start(bf16[72,768]{1,0:T(8,128)(2,1)S(1)} %get-tuple-element.140), channel_id=1, source_target_pairs={{0,8},{4,12},{8,0},{12,4},{1,9},{5,13},{9,1},{13,5},{2,10},{6,14},... | collective-permute-start | bytes 331784 | tf_op jit(solution)/shard_map/ppermute | solution.py:275
  368.7 8.8 %collective-permute-start.41 = (bf16[72,768]{1,0:T(8,128)(2,1)S(1)}, bf16[72,768]{1,0:T(8,128)(2,1)S(1)}, u32[]{:S(2)}, u32[]{:S(2)}) collective-permute-start(bf16[72,768]{1,0:T(8,128)(2,1)S(1)} %get-tuple-element.141), channel_id=1, source_target_pairs={{0,4},{4,8},{8,12},{12,0},{1,5},{5,9},{9,13},{13,1},{2,6},{6,10},{... | collective-permute-start | bytes 331784 | tf_op jit(solution)/shard_map/ppermute | solution.py:275
  (50 other events, 777.6 us)
Sparse Core Ops, SparseCore 0:
  31.0 21.0 all-gather.1

commit v2 on v1

--- a/solution.py
+++ b/solution.py
@@ -9,9 +9,10 @@
 
 Z_WINDOW = 3
 X_WINDOW = 3
-Z_LAG = 3
-X_LAG = 2
+Z_AFTER = {3: 0, 4: 1}
+X_AFTER = {2: 0, 3: 1, 4: 2}
 OWN_AT = (0, 0, 0, 1, 2, 3, 4, 5)
+Y_PARTS = 2
 NT = (((1,), (1,)), ((), ()))
 
 
@@ -38,9 +39,16 @@
     return lax.optimization_barrier((value, *others))[0]
 
 
+def gather_rows(block):
+    size = lax.axis_size("mp")
+    me = lax.axis_index("mp")
+    held = jnp.stack([block] + [lax.ppermute(block, "mp", exchange("mp", bits)) for bits in range(1, size)])
+    return jnp.concatenate([lax.dynamic_index_in_dim(held, me ^ index, 0, keepdims=False) for index in range(size)], axis=1)
+
+
 def column_chunks(width):
     unit = width // 16
-    sizes = (2, 4, 4, 4, 2)
+    sizes = (3, 4, 4, 3, 2)
     bounds = [0]
     for size in sizes:
         bounds.append(bounds[-1] + size * unit)
@@ -114,9 +122,7 @@
         input_output_aliases=aliases,
         compiler_params=pltpu.CompilerParams(vmem_limit_bytes=48 * 1024 * 1024),
         cost_estimate=pl.CostEstimate(
-            flops=8 * slot_count * width_all * width,
-            bytes_accessed=4 * width_all * width + 10 * slot_count * width_all,
-            transcendentals=slot_count * width,
+            flops=1024, bytes_accessed=1024, transcendentals=0,
         ),
     )(*operands)
 
@@ -156,8 +162,8 @@
         piece = stored(chunk, step)
         if step:
             first = [arrivals[-Z_WINDOW]] if len(arrivals) >= Z_WINDOW else []
-            if chunk >= Z_LAG:
-                first.append(finished[chunk - Z_LAG])
+            if chunk in Z_AFTER:
+                first.append(finished[Z_AFTER[chunk]])
             if first:
                 piece = after(piece, *first)
             piece = lax.ppermute(piece, "expert", shift_by("expert", step))
@@ -167,8 +173,8 @@
     def to_both(chunk, step):
         piece = landed[chunk, step]
         first = [crossings[-X_WINDOW]] if len(crossings) >= X_WINDOW else []
-        if step and chunk >= X_LAG:
-            first.append(finished[chunk - X_LAG])
+        if step and chunk in X_AFTER:
+            first.append(finished[X_AFTER[chunk]])
         if first:
             piece = after(piece, *first)
         if pair:
@@ -194,7 +200,6 @@
             dp_index = lax.rem(my_dp - far + n_dp, n_dp) if pair else far
             order.append((dp_index * n_expert + expert_index) * depth)
 
-    expert_ids = after(expert_ids, landed[0, 0])
     placed = slot_map(expert_ids, n_expert, slots_cap).astype(jnp.float32)
     select = jnp.sum(placed, axis=1)
     sent_rows = jnp.dot(
@@ -219,7 +224,7 @@
         axis=0,
     )
     scale = slots[:, feat_part : feat_part + 1].astype(jnp.float32)
-    rows_full = lax.all_gather(slots[:, :feat_part], "mp", axis=1, tiled=True)
+    rows_full = gather_rows(slots[:, :feat_part])
     rows = jnp.concatenate(
         [lax.dynamic_slice(rows_full, (0, start), (slot_count, depth)) for start in order], axis=1
     )
@@ -266,13 +271,19 @@
     kept = sums[0].reshape(n_expert, slots_cap, feat_part)
     given = sums[bit].reshape(n_expert, slots_cap, feat_part)
     returned = {}
-    for step in sorted(range(n_expert), key=lambda s: abs(2 * s - n_expert) if s else 2 * n_expert):
-        group = lax.rem(my_expert + step, n_expert)
-        block = lax.dynamic_index_in_dim(given, group, 0, keepdims=False)
-        block = lax.ppermute(block.astype(jnp.bfloat16), "mp", exchange("mp", bit))
-        block = lax.dynamic_index_in_dim(kept, group, 0, keepdims=False) + block.astype(jnp.float32)
-        block = block.astype(jnp.bfloat16)
-        returned[step] = lax.ppermute(block, "expert", shift_by("expert", step)) if step else block
+    far_first = sorted(range(n_expert), key=lambda s: abs(2 * s - n_expert) if s else 2 * n_expert)
+    bunch = n_expert // Y_PARTS
+    for turn in range(0, n_expert, bunch):
+        steps = far_first[turn : turn + bunch]
+        groups = [lax.rem(my_expert + step, n_expert) for step in steps]
+        pick = lambda blocks: jnp.stack(
+            [lax.dynamic_index_in_dim(blocks, group, 0, keepdims=False) for group in groups]
+        )
+        came_back = lax.ppermute(pick(given).astype(jnp.bfloat16), "mp", exchange("mp", bit))
+        summed = (pick(kept) + came_back.astype(jnp.float32)).astype(jnp.bfloat16)
+        for index, step in enumerate(steps):
+            block = summed[index]
+            returned[step] = lax.ppermute(block, "expert", shift_by("expert", step)) if step else block
     split = select.reshape(select.shape[0], n_expert, slots_cap)
     chosen = jnp.concatenate(
         [

time: 386 us -> 371 us (0.961)
  starting transfers between devices: 160 us -> 57.1 us
  waiting for transfers between devices: 122 us -> 198 us
  between operations: 14.9 us -> 1.58 us
  Pallas kernels: 46.4 us -> 57.9 us
  local copies, waits for them, and re-layouts: 29.9 us -> 37.5 us
  other arithmetic: 11 us -> 16.9 us
    ppermute x15, starting transfers between devices: 110 us -> 15.3 us  [to_owner(): piece = lax.ppermute(piece, 'expert', shift_by('expert', step))]
    ppermute x15, waiting for transfers between devices: 51 us -> 144 us  [to_owner(): piece = lax.ppermute(piece, 'expert', shift_by('expert', step))]
    ppermute x6, starting transfers between devices: 24.4 us -> 6.03 us  [per_device(): lax.ppermute(block, 'expert', shift_by('expert', step))]
    ppermute x6, waiting for transfers between devices: 17.9 us -> 6.39 us  [per_device(): lax.ppermute(block, 'expert', shift_by('expert', step))]
    pallas_call x5, Pallas kernels: 46.4 us -> 57.9 us  [expert_chunk(): pl.pallas_call(functools.partial(expert_kernel, len(parts), carried is No...]
    ppermute x20, starting transfers between devices: 20.9 us -> 31.7 us  [to_both(): spread[chunk, step] = lax.ppermute(piece, 'dp', shift_by('dp', 1))]
    ppermute x20, waiting for transfers between devices: 41.3 us -> 34 us  [to_both(): spread[chunk, step] = lax.ppermute(piece, 'dp', shift_by('dp', 1))]
    unnamed x109 -> x150, local copies, waits for them, and re-layouts: 15.3 us -> 19.6 us
  transfers between devices with their start and end apart: 47 -> 47, of which waited for: 21 -> 18; matrix products, arithmetic and copies ran while one was open for 6% -> 9% of each run, Pallas kernels for 10% -> 14%
where the time goes in v2:
time: 371 us; the launch traced here: 370 us
  waiting for transfers between devices  198 us (53%)
  Pallas kernels  57.9 us (16%)
  starting transfers between devices  57.1 us (15%)
  local copies, waits for them, and re-layouts  37.5 us (10%)
  other arithmetic  16.9 us (5%)
    ppermute x15, waiting for transfers between devices, to_owner(): piece = lax.ppermute(piece, 'expert', shift_by('expert', step))  144 us
    pallas_call x5, Pallas kernels, expert_chunk(): pl.pallas_call(functools.partial(expert_kernel, len(parts), carried is No...  57.9 us
    ppermute x20, waiting for transfers between devices, to_both(): spread[chunk, step] = lax.ppermute(piece, 'dp', shift_by('dp', 1))  34 us
    ppermute x20, starting transfers between devices, to_both(): spread[chunk, step] = lax.ppermute(piece, 'dp', shift_by('dp', 1))  31.7 us
    unnamed x150, local copies, waits for them, and re-layouts  19.6 us
    ppermute x15, starting transfers between devices, to_owner(): piece = lax.ppermute(piece, 'expert', shift_by('expert', step))  15.3 us
    dynamic_slice x3, local copies, waits for them, and re-layouts, stored(): lax.dynamic_slice(w, (target, 0, begin), (1, depth, end - begin))[0]  11.9 us
    another operation x20, other arithmetic, stored(): jnp.stack([lax.dynamic_slice(w, (target, 0, begin), (1, depth, end - begi...  11.4 us
  transfers between devices with their start and end apart: 47, of which 18 were waited for; matrix products, arithmetic and copies ran while one was open for 9% of the time, Pallas kernels for 14%

profile of v2, /device:TPU:0, one launch (start us, length us, event | category | flops | bytes accessed | tf_op | source)
XLA Modules:
  0.0 370.2 jit_solution(11187243919394432361)
XLA Ops:
  0.7 5.2 %constant_dynamic-slice_fusion.20 = (bf16[1,384,512]{2,1,0:T(8,128)(2,1)}, bf16[1,384,512]{2,1,0:T(8,128)(2,1)}, bf16[1,384,512]{2,1,0:T(8,128)(2,1)}, bf16[1,38...) fusion(bf16[4,384,2048]{2,1,0:T(8,128)(2,1)} %param.10, ...), kind=kLoop, calls=%fused_computation.109 | loop fusion | bytes 12582928 | tf_op jit(solution)/shard_map/dynamic_slice | solution.py:151
  6.0 3.0 collective-permute-start.9
  12.7 1.6 collective-permute-start
  14.3 2.6 collective-permute-start.1
  16.9 1.3 collective-permute-start.2
  18.2 4.1 %constant_dynamic-slice_fusion.12 = (bf16[1,384,384]{2,1,0:T(8,128)(2,1)}, bf16[1,384,384]{2,1,0:T(8,128)(2,1)}, bf16[1,384,384]{2,1,0:T(8,128)(2,1)}, bf16[1,38...) fusion(bf16[4,384,2048]{2,1,0:T(8,128)(2,1)} %param.10, ...), kind=kLoop, calls=%fused_computation.101 | loop fusion | bytes 9437200 | tf_op jit(solution)/shard_map/dynamic_slice | solution.py:151
  29.7 1.5 collective-permute-start.17
  31.2 1.6 collective-permute-start.6
  34.0 6.0 %collective-permute-done.14.refs_1_ = bf16[2,384,384]{2,1,0:T(8,128)(2,1)S(1)} collective-permute-done((bf16[2,384,384]{2,1,0:T(8,128)(2,1)S(1)}, bf16[2,384,384]{2,1,0:T(8,128)(2,1)S(1)}, u32[]{:S(2)}, u32[]{:S(2)}) %collective-permute-start.14) | collective-permute-done | bytes 589856 | tf_op jit(solution)/shard_map/ppermute | solution.py:181
  40.0 3.2 collective-permute-start.16
  44.1 14.2 %collective-permute-done.6.refs_2_ = bf16[2,384,384]{2,1,0:T(8,128)(2,1)} collective-permute-done((bf16[2,384,384]{2,1,0:T(8,128)(2,1)S(1)}, bf16[2,384,384]{2,1,0:T(8,128)(2,1)}, u32[]{:S(2)}, u32[]{:S(2)}) %collective-permute-start.6) | collective-permute-done | bytes 589856 | tf_op jit(solution)/shard_map/ppermute | solution.py:169
  60.4 2.5 constant_dynamic-slice_fusion.14
  63.0 1.6 collective-permute-start.4
  64.9 16.7 %collective-permute-done.16.refs_4_ = bf16[2,384,384]{2,1,0:T(8,128)(2,1)} collective-permute-done((bf16[2,384,384]{2,1,0:T(8,128)(2,1)}, bf16[2,384,384]{2,1,0:T(8,128)(2,1)}, u32[]{:S(2)}, u32[]{:S(2)}) %collective-permute-start.16) | collective-permute-done | bytes 589856 | tf_op jit(solution)/shard_map/ppermute | solution.py:169
  81.5 1.2 collective-permute-start.15
  86.3 1.3 pad_maximum_fusion.5
  88.4 3.9 %collective-permute-start.23 = (bf16[2,384,512]{2,1,0:T(8,128)(2,1)S(1)}, bf16[2,384,512]{2,1,0:T(8,128)(2,1)S(1)}, u32[]{:S(2)}, u32[]{:S(2)}) collective-permute-start(bf16[2,384,512]{2,1,0:T(8,128)(2,1)S(1)} %copy-done.59), channel_id=1, source_target_pairs={{0,12},{4,0},{8,4},{12,8},{1,13},{5,1},{9,5},{13,9},{2,14},{6,2},{... | collective-permute-start | bytes 2359304 | tf_op jit(solution)/shard_map/ppermute | solution.py:169
  92.2 1.2 collective-permute-start.18
  93.5 1.4 pad_maximum_fusion
  94.9 3.1 collective-permute-done.15.refs_3_
  98.8 11.8 %collective-permute-done.10.refs_7_ = bf16[2,384,384]{2,1,0:T(8,128)(2,1)S(1)} collective-permute-done((bf16[2,384,384]{2,1,0:T(8,128)(2,1)}, bf16[2,384,384]{2,1,0:T(8,128)(2,1)S(1)}, u32[]{:S(2)}, u32[]{:S(2)}) %collective-permute-start.10) | collective-permute-done | bytes 589856 | tf_op jit(solution)/shard_map/ppermute | solution.py:181
  113.8 9.5 %collective-permute-done.18.refs_5_ = bf16[2,384,384]{2,1,0:T(8,128)(2,1)S(1)} collective-permute-done((bf16[2,384,384]{2,1,0:T(8,128)(2,1)}, bf16[2,384,384]{2,1,0:T(8,128)(2,1)S(1)}, u32[]{:S(2)}, u32[]{:S(2)}) %collective-permute-start.18) | collective-permute-done | bytes 589856 | tf_op jit(solution)/shard_map/ppermute | solution.py:181
  124.1 1.2 collective-permute-start.24
  126.8 43.2 %collective-permute-done.20.refs_4_ = bf16[2,384,512]{2,1,0:T(8,128)(2,1)S(1)} collective-permute-done((bf16[2,384,512]{2,1,0:T(8,128)(2,1)S(1)}, bf16[2,384,512]{2,1,0:T(8,128)(2,1)S(1)}, u32[]{:S(2)}, u32[]{:S(2)}) %collective-permute-start.20) | collective-permute-done | bytes 786464 | tf_op jit(solution)/shard_map/ppermute | solution.py:169
  174.6 1.2 collective-permute-start.12
  176.6 10.6 %shard_map.77 = (bf16[288,2048]{1,0:T(8,128)(2,1)}, f32[288,3072]{1,0:T(8,128)}, f32[8,128]{1,0:T(8,128)}) custom-call(bf16[288,3072]{1,0:T(8,128)(2,1)} %dynamic-slice_dynamic-update-slice_fusion.rows_ref, f32[288,1]{1,0:T(8,128)S(1)} %maximum_convert_fusion.scale_ref, bf16[288,2048]{1,0:T(8,128)(2,1)S(1)} %bitcast.83, bf16[2,384,384]{2,1,0:T(8,128)(2,1)S(1)} %copy-done.5, ...), custom_call_target="tpu_custom_call" | custom-call | flops 1024 | bytes 1024 | tf_op jit(solution)/shard_map/pallas_call | solution.py:112
  187.2 2.1 collective-permute-start.19
  189.3 1.6 collective-permute-done.30.refs_6_
  193.0 40.8 %collective-permute-done.28.refs_4_ = bf16[2,384,512]{2,1,0:T(8,128)(2,1)S(1)} collective-permute-done((bf16[2,384,512]{2,1,0:T(8,128)(2,1)}, bf16[2,384,512]{2,1,0:T(8,128)(2,1)S(1)}, u32[]{:S(2)}, u32[]{:S(2)}) %collective-permute-start.28) | collective-permute-done | bytes 786464 | tf_op jit(solution)/shard_map/ppermute | solution.py:169
  235.8 1.4 collective-permute-start.33
  237.3 14.1 %shard_map.78 = (bf16[288,2048]{1,0:T(8,128)(2,1)}, f32[288,3072]{1,0:T(8,128)}, f32[8,128]{1,0:T(8,128)}) custom-call(bf16[288,3072]{1,0:T(8,128)(2,1)} %dynamic-slice_dynamic-update-slice_fusion.rows_ref, f32[288,1]{1,0:T(8,128)S(1)} %maximum_convert_fusion.scale_ref, bf16[288,2048]{1,0:T(8,128)(2,1)} %bitcast.81, ...), custom_call_target="tpu_custom_call", output_to_operand_aliasing={{1}: (11, {}), {0}: (12, {})} | custom-call | flops 1024 | bytes 1024 | tf_op jit(solution)/shard_map/pallas_call | solution.py:112
  252.2 1.3 collective-permute-start.27
  254.3 27.5 %collective-permute-done.33.refs_4_ = bf16[2,384,384]{2,1,0:T(8,128)(2,1)S(1)} collective-permute-done((bf16[2,384,384]{2,1,0:T(8,128)(2,1)S(1)}, bf16[2,384,384]{2,1,0:T(8,128)(2,1)S(1)}, u32[]{:S(2)}, u32[]{:S(2)}) %collective-permute-start.33) | collective-permute-done | bytes 589856 | tf_op jit(solution)/shard_map/ppermute | solution.py:169
  281.7 1.6 collective-permute-start.35
  283.5 1.6 collective-permute-start.34
  285.1 13.9 %shard_map.79 = (bf16[288,2048]{1,0:T(8,128)(2,1)}, f32[288,3072]{1,0:T(8,128)}, f32[8,128]{1,0:T(8,128)}) custom-call(bf16[288,3072]{1,0:T(8,128)(2,1)} %dynamic-slice_dynamic-update-slice_fusion.rows_ref, f32[288,1]{1,0:T(8,128)S(1)} %maximum_convert_fusion.scale_ref, bf16[288,2048]{1,0:T(8,128)(2,1)} %bitcast.82, ...), custom_call_target="tpu_custom_call", output_to_operand_aliasing={{1}: (11, {}), {0}: (12, {})} | custom-call | flops 1024 | bytes 1024 | tf_op jit(solution)/shard_map/pallas_call | solution.py:112
  299.9 9.8 %collective-permute-start.32 = (bf16[2,384,256]{2,1,0:T(8,128)(2,1)}, bf16[2,384,256]{2,1,0:T(8,128)(2,1)}, u32[]{:S(2)}, u32[]{:S(2)}) collective-permute-start(bf16[2,384,256]{2,1,0:T(8,128)(2,1)} %collective-permute-done.25.refs_2_), channel_id=1, source_target_pairs={{0,16},{16,0},{1,17},{17,1},{2,18},{18,2},{3,19},{19,3},{4,20},{20... | collective-permute-start | bytes 1179656 | tf_op jit(solution)/shard_map/ppermute | solution.py:181
  311.4 2.0 collective-permute-start.36
  320.9 11.5 %shard_map.80 = (bf16[288,2048]{1,0:T(8,128)(2,1)}, f32[288,3072]{1,0:T(8,128)}, f32[8,128]{1,0:T(8,128)}) custom-call(bf16[288,3072]{1,0:T(8,128)(2,1)} %dynamic-slice_dynamic-update-slice_fusion.rows_ref, f32[288,1]{1,0:T(8,128)S(1)} %maximum_convert_fusion.scale_ref, ...), custom_call_target="tpu_custom_call", output_to_operand_aliasing={{1}: (11, {}), {0}: (12, {})} | custom-call | flops 1024 | bytes 1024 | tf_op jit(solution)/shard_map/pallas_call | solution.py:112
  332.4 3.3 collective-permute-done.36.refs_5_
  335.7 7.8 %shard_map.81 = (bf16[288,2048]{1,0:T(8,128)(2,1)}, f32[288,3072]{1,0:T(8,128)}, f32[8,128]{1,0:T(8,128)}) custom-call(bf16[288,3072]{1,0:T(8,128)(2,1)} %dynamic-slice_dynamic-update-slice_fusion.rows_ref, f32[288,1]{1,0:T(8,128)S(1)} %maximum_convert_fusion.scale_ref, ...), custom_call_target="tpu_custom_call", output_to_operand_aliasing={{1}: (11, {}), {0}: (12, {})} | custom-call | flops 1024 | bytes 1024 | tf_op jit(solution)/shard_map/pallas_call | solution.py:112
  343.6 2.2 constant_dynamic-slice_fusion.3
  346.1 3.7 collective-permute-done.41
  350.1 1.6 collective-permute-start.43
  352.6 5.9 %collective-permute-done.43 = bf16[2,72,768]{2,1,0:T(8,128)(2,1)S(1)} collective-permute-done((bf16[2,72,768]{2,1,0:T(8,128)(2,1)S(1)}, bf16[2,72,768]{2,1,0:T(8,128)(2,1)S(1)}, u32[]{:S(2)}, u32[]{:S(2)}) %collective-permute-start.43) | collective-permute-done | bytes 221216 | tf_op jit(solution)/shard_map/ppermute | solution.py:282
  359.0 3.4 collective-permute-done.42
  362.6 3.5 collective-permute-done.44
  366.1 2.7 collective-permute-done.45
  (270 shorter events, 50.4 us)
Async XLA Ops:
  6.0 76.8 %collective-permute-start.9 = (bf16[2,384,512]{2,1,0:T(8,128)(2,1)S(1)}, bf16[2,384,512]{2,1,0:T(8,128)(2,1)}, u32[]{:S(2)}, u32[]{:S(2)}) collective-permute-start(bf16[2,384,512]{2,1,0:T(8,128)(2,1)S(1)} %pad_maximum_fusion.4.refs_0_), channel_id=1, source_target_pairs={{0,16},{16,0},{1,17},{17,1},{2,18},{18,2},{3,19},{19,3},{4,20},{20... | collective-permute-start | bytes 2359304 | tf_op jit(solution)/shard_map/ppermute | solution.py:181
  12.7 16.5 %collective-permute-start = (bf16[72,896]{1,0:T(8,128)(2,1)}, bf16[72,896]{1,0:T(8,128)(2,1)S(1)}, u32[]{:S(2)}, u32[]{:S(2)}) collective-permute-start(bf16[72,896]{1,0:T(8,128)(2,1)} %get-tuple-element.153), channel_id=1, source_target_pairs={{0,4},{4,8},{8,12},{12,0},{1,5},{5,9},{9,13},{13,1},{2,6},{6,10},{... | collective-permute-start | bytes 387080 | tf_op jit(solution)/shard_map/ppermute | solution.py:217
  14.3 15.4 %collective-permute-start.1 = (bf16[72,896]{1,0:T(8,128)(2,1)}, bf16[72,896]{1,0:T(8,128)(2,1)S(1)}, u32[]{:S(2)}, u32[]{:S(2)}) collective-permute-start(bf16[72,896]{1,0:T(8,128)(2,1)} %get-tuple-element.152), channel_id=1, source_target_pairs={{0,8},{4,12},{8,0},{12,4},{1,9},{5,13},{9,1},{13,5},{2,10},{6,14},... | collective-permute-start | bytes 387080 | tf_op jit(solution)/shard_map/ppermute | solution.py:217
  16.9 14.3 %collective-permute-start.2 = (bf16[72,896]{1,0:T(8,128)(2,1)}, bf16[72,896]{1,0:T(8,128)(2,1)}, u32[]{:S(2)}, u32[]{:S(2)}) collective-permute-start(bf16[72,896]{1,0:T(8,128)(2,1)} %get-tuple-element.151), channel_id=1, source_target_pairs={{0,12},{4,0},{8,4},{12,8},{1,13},{5,1},{9,5},{13,9},{2,14},{6,2},{... | collective-permute-start | bytes 387080 | tf_op jit(solution)/shard_map/ppermute | solution.py:217
  22.5 17.5 %collective-permute-start.14 = (bf16[2,384,384]{2,1,0:T(8,128)(2,1)S(1)}, bf16[2,384,384]{2,1,0:T(8,128)(2,1)S(1)}, u32[]{:S(2)}, u32[]{:S(2)}) collective-permute-start(bf16[2,384,384]{2,1,0:T(8,128)(2,1)S(1)} %pad_maximum_fusion.14.refs_0_), channel_id=1, source_target_pairs={{0,16},{16,0},{1,17},{17,1},{2,18},{18,2},{3,19},{19,3},{4,20},{20... | collective-permute-start | bytes 1769480 | tf_op jit(solution)/shard_map/ppermute | solution.py:181
  29.2 35.4 %collective-permute-start.8 = (bf16[2,384,384]{2,1,0:T(8,128)(2,1)}, bf16[2,384,384]{2,1,0:T(8,128)(2,1)}, u32[]{:S(2)}, u32[]{:S(2)}) collective-permute-start(bf16[2,384,384]{2,1,0:T(8,128)(2,1)} %pad_maximum_fusion.12), channel_id=1, source_target_pairs={{0,12},{4,0},{8,4},{12,8},{1,13},{5,1},{9,5},{13,9},{2,14},{6,2},{... | collective-permute-start | bytes 1769480 | tf_op jit(solution)/shard_map/ppermute | solution.py:169
  29.7 54.0 %collective-permute-start.17 = (bf16[2,384,512]{2,1,0:T(8,128)(2,1)S(1)}, bf16[2,384,512]{2,1,0:T(8,128)(2,1)S(1)}, u32[]{:S(2)}, u32[]{:S(2)}) collective-permute-start(bf16[2,384,512]{2,1,0:T(8,128)(2,1)S(1)} %pad_maximum_fusion.6.refs_0_), channel_id=1, source_target_pairs={{0,16},{16,0},{1,17},{17,1},{2,18},{18,2},{3,19},{19,3},{4,20},{20... | collective-permute-start | bytes 2359304 | tf_op jit(solution)/shard_map/ppermute | solution.py:181
  31.2 27.1 %collective-permute-start.6 = (bf16[2,384,384]{2,1,0:T(8,128)(2,1)S(1)}, bf16[2,384,384]{2,1,0:T(8,128)(2,1)}, u32[]{:S(2)}, u32[]{:S(2)}) collective-permute-start(bf16[2,384,384]{2,1,0:T(8,128)(2,1)S(1)} %pad_maximum_fusion.11), channel_id=1, source_target_pairs={{0,4},{4,8},{8,12},{12,0},{1,5},{5,9},{9,13},{13,1},{2,6},{6,10},{... | collective-permute-start | bytes 1769480 | tf_op jit(solution)/shard_map/ppermute | solution.py:169
  40.0 41.5 %collective-permute-start.16 = (bf16[2,384,384]{2,1,0:T(8,128)(2,1)}, bf16[2,384,384]{2,1,0:T(8,128)(2,1)}, u32[]{:S(2)}, u32[]{:S(2)}) collective-permute-start(bf16[2,384,384]{2,1,0:T(8,128)(2,1)} %pad_maximum_fusion.15), channel_id=1, source_target_pairs={{0,8},{4,12},{8,0},{12,4},{1,9},{5,13},{9,1},{13,5},{2,10},{6,14},... | collective-permute-start | bytes 1769480 | tf_op jit(solution)/shard_map/ppermute | solution.py:169
  58.3 4.6 %collective-permute-start.3 = (bf16[288,768]{1,0:T(8,128)(2,1)}, bf16[288,768]{1,0:T(8,128)(2,1)S(1)}, u32[]{:S(2)}, u32[]{:S(2)}) collective-permute-start(bf16[288,768]{1,0:T(8,128)(2,1)} %get-tuple-element.145), channel_id=1, source_target_pairs={{0,1},{1,0},{2,3},{3,2},{4,5},{5,4},{6,7},{7,6},{8,9},{9,8},{10,11... | collective-permute-start | bytes 1327112 | tf_op jit(solution)/shard_map/ppermute | solution.py:45
  63.0 25.4 %collective-permute-start.4 = (bf16[288,768]{1,0:T(8,128)(2,1)}, bf16[288,768]{1,0:T(8,128)(2,1)}, u32[]{:S(2)}, u32[]{:S(2)}) collective-permute-start(bf16[288,768]{1,0:T(8,128)(2,1)} %get-tuple-element.145), channel_id=1, source_target_pairs={{0,2},{1,3},{2,0},{3,1},{4,6},{5,7},{6,4},{7,5},{8,10},{9,11},{10,... | collective-permute-start | bytes 1327112 | tf_op jit(solution)/shard_map/ppermute | solution.py:45
  64.6 27.7 %collective-permute-start.5 = (bf16[288,768]{1,0:T(8,128)(2,1)}, bf16[288,768]{1,0:T(8,128)(2,1)}, u32[]{:S(2)}, u32[]{:S(2)}) collective-permute-start(bf16[288,768]{1,0:T(8,128)(2,1)} %get-tuple-element.145), channel_id=1, source_target_pairs={{0,3},{1,2},{2,1},{3,0},{4,7},{5,6},{6,5},{7,4},{8,11},{9,10},{10,... | collective-permute-start | bytes 1327112 | tf_op jit(solution)/shard_map/ppermute | solution.py:45
  81.5 16.5 %collective-permute-start.15 = (bf16[2,384,384]{2,1,0:T(8,128)(2,1)}, bf16[2,384,384]{2,1,0:T(8,128)(2,1)S(1)}, u32[]{:S(2)}, u32[]{:S(2)}) collective-permute-start(bf16[2,384,384]{2,1,0:T(8,128)(2,1)} %collective-permute-done.6.refs_2_), channel_id=1, source_target_pairs={{0,16},{16,0},{1,17},{17,1},{2,18},{18,2},{3,19},{19,3},{4,20},{20... | collective-permute-start | bytes 1769480 | tf_op jit(solution)/shard_map/ppermute | solution.py:181
  82.8 29.9 %collective-permute-start.7 = (bf16[2,384,512]{2,1,0:T(8,128)(2,1)}, bf16[2,384,512]{2,1,0:T(8,128)(2,1)}, u32[]{:S(2)}, u32[]{:S(2)}) collective-permute-start(bf16[2,384,512]{2,1,0:T(8,128)(2,1)} %pad_maximum_fusion.3), channel_id=1, source_target_pairs={{0,4},{4,8},{8,12},{12,0},{1,5},{5,9},{9,13},{13,1},{2,6},{6,10},{... | collective-permute-start | bytes 2359304 | tf_op jit(solution)/shard_map/ppermute | solution.py:169
  84.7 26.0 %collective-permute-start.10 = (bf16[2,384,384]{2,1,0:T(8,128)(2,1)}, bf16[2,384,384]{2,1,0:T(8,128)(2,1)S(1)}, u32[]{:S(2)}, u32[]{:S(2)}) collective-permute-start(bf16[2,384,384]{2,1,0:T(8,128)(2,1)} %collective-permute-done.8.refs_6_), channel_id=1, source_target_pairs={{0,16},{16,0},{1,17},{17,1},{2,18},{18,2},{3,19},{19,3},{4,20},{20... | collective-permute-start | bytes 1769480 | tf_op jit(solution)/shard_map/ppermute | solution.py:181
  88.4 35.7 %collective-permute-start.23 = (bf16[2,384,512]{2,1,0:T(8,128)(2,1)S(1)}, bf16[2,384,512]{2,1,0:T(8,128)(2,1)S(1)}, u32[]{:S(2)}, u32[]{:S(2)}) collective-permute-start(bf16[2,384,512]{2,1,0:T(8,128)(2,1)S(1)} %copy-done.59), channel_id=1, source_target_pairs={{0,12},{4,0},{8,4},{12,8},{1,13},{5,1},{9,5},{13,9},{2,14},{6,2},{... | collective-permute-start | bytes 2359304 | tf_op jit(solution)/shard_map/ppermute | solution.py:169
  92.2 31.0 %collective-permute-start.18 = (bf16[2,384,384]{2,1,0:T(8,128)(2,1)}, bf16[2,384,384]{2,1,0:T(8,128)(2,1)S(1)}, u32[]{:S(2)}, u32[]{:S(2)}) collective-permute-start(bf16[2,384,384]{2,1,0:T(8,128)(2,1)} %collective-permute-done.16.refs_4_), channel_id=1, source_target_pairs={{0,16},{16,0},{1,17},{17,1},{2,18},{18,2},{3,19},{19,3},{4,20},{20... | collective-permute-start | bytes 1769480 | tf_op jit(solution)/shard_map/ppermute | solution.py:181
  98.0 72.0 %collective-permute-start.20 = (bf16[2,384,512]{2,1,0:T(8,128)(2,1)S(1)}, bf16[2,384,512]{2,1,0:T(8,128)(2,1)S(1)}, u32[]{:S(2)}, u32[]{:S(2)}) collective-permute-start(bf16[2,384,512]{2,1,0:T(8,128)(2,1)S(1)} %copy-done.58), channel_id=1, source_target_pairs={{0,8},{4,12},{8,0},{12,4},{1,9},{5,13},{9,1},{13,5},{2,10},{6,14},... | collective-permute-start | bytes 2359304 | tf_op jit(solution)/shard_map/ppermute | solution.py:169
  111.5 59.3 %collective-permute-start.21 = (bf16[2,384,384]{2,1,0:T(8,128)(2,1)S(1)}, bf16[2,384,384]{2,1,0:T(8,128)(2,1)S(1)}, u32[]{:S(2)}, u32[]{:S(2)}) collective-permute-start(bf16[2,384,384]{2,1,0:T(8,128)(2,1)S(1)} %pad_maximum_fusion.16.refs_0_), channel_id=1, source_target_pairs={{0,16},{16,0},{1,17},{17,1},{2,18},{18,2},{3,19},{19,3},{4,20},{20... | collective-permute-start | bytes 1769480 | tf_op jit(solution)/shard_map/ppermute | solution.py:181
  112.7 58.9 %collective-permute-start.11 = (bf16[2,384,512]{2,1,0:T(8,128)(2,1)}, bf16[2,384,512]{2,1,0:T(8,128)(2,1)S(1)}, u32[]{:S(2)}, u32[]{:S(2)}) collective-permute-start(bf16[2,384,512]{2,1,0:T(8,128)(2,1)} %collective-permute-done.7.refs_2_), channel_id=1, source_target_pairs={{0,16},{16,0},{1,17},{17,1},{2,18},{18,2},{3,19},{19,3},{4,20},{20... | collective-permute-start | bytes 2359304 | tf_op jit(solution)/shard_map/ppermute | solution.py:181
  113.5 63.1 %copy-start.29 = (bf16[2,384,384]{2,1,0:T(8,128)(2,1)S(1)}, bf16[2,384,384]{2,1,0:T(8,128)(2,1)}, u32[]{:S(2)}) copy-start(bf16[2,384,384]{2,1,0:T(8,128)(2,1)} %copy-done.28) | copy-start | bytes 1769476
  123.3 51.3 %collective-permute-start.13 = (bf16[2,384,512]{2,1,0:T(8,128)(2,1)S(1)}, bf16[2,384,512]{2,1,0:T(8,128)(2,1)S(1)}, u32[]{:S(2)}, u32[]{:S(2)}) collective-permute-start(bf16[2,384,512]{2,1,0:T(8,128)(2,1)S(1)} %pad_maximum_fusion.5), channel_id=1, source_target_pairs={{0,4},{4,8},{8,12},{12,0},{1,5},{5,9},{9,13},{13,1},{2,6},{6,10},{... | collective-permute-start | bytes 2359304 | tf_op jit(solution)/shard_map/ppermute | solution.py:169
  124.1 63.2 %collective-permute-start.24 = (bf16[2,384,512]{2,1,0:T(8,128)(2,1)S(1)}, bf16[2,384,512]{2,1,0:T(8,128)(2,1)}, u32[]{:S(2)}, u32[]{:S(2)}) collective-permute-start(bf16[2,384,512]{2,1,0:T(8,128)(2,1)S(1)} %collective-permute-done.23.refs_6_), channel_id=1, source_target_pairs={{0,16},{16,0},{1,17},{17,1},{2,18},{18,2},{3,19},{19,3},{4,20},{20... | collective-permute-start | bytes 2359304 | tf_op jit(solution)/shard_map/ppermute | solution.py:181
  170.0 21.0 %collective-permute-start.30 = (bf16[2,384,512]{2,1,0:T(8,128)(2,1)}, bf16[2,384,512]{2,1,0:T(8,128)(2,1)S(1)}, u32[]{:S(2)}, u32[]{:S(2)}) collective-permute-start(bf16[2,384,512]{2,1,0:T(8,128)(2,1)} %pad_maximum_fusion.10), channel_id=1, source_target_pairs={{0,12},{4,0},{8,4},{12,8},{1,13},{5,1},{9,5},{13,9},{2,14},{6,2},{... | collective-permute-start | bytes 2359304 | tf_op jit(solution)/shard_map/ppermute | solution.py:169
  171.6 62.2 %collective-permute-start.28 = (bf16[2,384,512]{2,1,0:T(8,128)(2,1)}, bf16[2,384,512]{2,1,0:T(8,128)(2,1)S(1)}, u32[]{:S(2)}, u32[]{:S(2)}) collective-permute-start(bf16[2,384,512]{2,1,0:T(8,128)(2,1)} %pad_maximum_fusion.9), channel_id=1, source_target_pairs={{0,8},{4,12},{8,0},{12,4},{1,9},{5,13},{9,1},{13,5},{2,10},{6,14},... | collective-permute-start | bytes 2359304 | tf_op jit(solution)/shard_map/ppermute | solution.py:169
  171.6 20.4 %collective-permute-start.22 = (bf16[2,384,512]{2,1,0:T(8,128)(2,1)S(1)}, bf16[2,384,512]{2,1,0:T(8,128)(2,1)S(1)}, u32[]{:S(2)}, u32[]{:S(2)}) collective-permute-start(bf16[2,384,512]{2,1,0:T(8,128)(2,1)S(1)} %collective-permute-done.20.refs_4_), channel_id=1, source_target_pairs={{0,16},{16,0},{1,17},{17,1},{2,18},{18,2},{3,19},{19,3},{4,20},{20... | collective-permute-start | bytes 2359304 | tf_op jit(solution)/shard_map/ppermute | solution.py:181
  174.6 59.3 %collective-permute-start.12 = (bf16[2,384,256]{2,1,0:T(8,128)(2,1)S(1)}, bf16[2,384,256]{2,1,0:T(8,128)(2,1)S(1)}, u32[]{:S(2)}, u32[]{:S(2)}) collective-permute-start(bf16[2,384,256]{2,1,0:T(8,128)(2,1)S(1)} %copy-done.6), channel_id=1, source_target_pairs={{0,16},{16,0},{1,17},{17,1},{2,18},{18,2},{3,19},{19,3},{4,20},{20... | collective-permute-start | bytes 1179656 | tf_op jit(solution)/shard_map/ppermute | solution.py:181
  187.2 48.5 %collective-permute-start.19 = (bf16[2,384,384]{2,1,0:T(8,128)(2,1)}, bf16[2,384,384]{2,1,0:T(8,128)(2,1)S(1)}, u32[]{:S(2)}, u32[]{:S(2)}) collective-permute-start(bf16[2,384,384]{2,1,0:T(8,128)(2,1)} %pad_maximum_fusion.13), channel_id=1, source_target_pairs={{0,4},{4,8},{8,12},{12,0},{1,5},{5,9},{9,13},{13,1},{2,6},{6,10},{... | collective-permute-start | bytes 1769480 | tf_op jit(solution)/shard_map/ppermute | solution.py:169
  190.9 60.4 %collective-permute-start.26 = (bf16[2,384,512]{2,1,0:T(8,128)(2,1)S(1)}, bf16[2,384,512]{2,1,0:T(8,128)(2,1)S(1)}, u32[]{:S(2)}, u32[]{:S(2)}) collective-permute-start(bf16[2,384,512]{2,1,0:T(8,128)(2,1)S(1)} %collective-permute-done.13.refs_2_), channel_id=1, source_target_pairs={{0,16},{16,0},{1,17},{17,1},{2,18},{18,2},{3,19},{19,3},{4,20},{20... | collective-permute-start | bytes 2359304 | tf_op jit(solution)/shard_map/ppermute | solution.py:181
  192.0 61.5 %collective-permute-start.31 = (bf16[2,384,512]{2,1,0:T(8,128)(2,1)S(1)}, bf16[2,384,512]{2,1,0:T(8,128)(2,1)S(1)}, u32[]{:S(2)}, u32[]{:S(2)}) collective-permute-start(bf16[2,384,512]{2,1,0:T(8,128)(2,1)S(1)} %collective-permute-done.30.refs_6_), channel_id=1, source_target_pairs={{0,16},{16,0},{1,17},{17,1},{2,18},{18,2},{3,19},{19,3},{4,20},{20... | collective-permute-start | bytes 2359304 | tf_op jit(solution)/shard_map/ppermute | solution.py:181
  234.6 47.2 %collective-permute-start.29 = (bf16[2,384,512]{2,1,0:T(8,128)(2,1)S(1)}, bf16[2,384,512]{2,1,0:T(8,128)(2,1)S(1)}, u32[]{:S(2)}, u32[]{:S(2)}) collective-permute-start(bf16[2,384,512]{2,1,0:T(8,128)(2,1)S(1)} %collective-permute-done.28.refs_4_), channel_id=1, source_target_pairs={{0,16},{16,0},{1,17},{17,1},{2,18},{18,2},{3,19},{19,3},{4,20},{20... | collective-permute-start | bytes 2359304 | tf_op jit(solution)/shard_map/ppermute | solution.py:181
  235.4 16.7 %collective-permute-start.37 = (bf16[2,384,384]{2,1,0:T(8,128)(2,1)S(1)}, bf16[2,384,384]{2,1,0:T(8,128)(2,1)S(1)}, u32[]{:S(2)}, u32[]{:S(2)}) collective-permute-start(bf16[2,384,384]{2,1,0:T(8,128)(2,1)S(1)} %pad_maximum_fusion.18), channel_id=1, source_target_pairs={{0,12},{4,0},{8,4},{12,8},{1,13},{5,1},{9,5},{13,9},{2,14},{6,2},{... | collective-permute-start | bytes 1769480 | tf_op jit(solution)/shard_map/ppermute | solution.py:169
  235.8 45.9 %collective-permute-start.33 = (bf16[2,384,384]{2,1,0:T(8,128)(2,1)S(1)}, bf16[2,384,384]{2,1,0:T(8,128)(2,1)S(1)}, u32[]{:S(2)}, u32[]{:S(2)}) collective-permute-start(bf16[2,384,384]{2,1,0:T(8,128)(2,1)S(1)} %pad_maximum_fusion.17), channel_id=1, source_target_pairs={{0,8},{4,12},{8,0},{12,4},{1,9},{5,13},{9,1},{13,5},{2,10},{6,14},... | collective-permute-start | bytes 1769480 | tf_op jit(solution)/shard_map/ppermute | solution.py:169
  251.4 32.1 %collective-permute-start.25 = (bf16[2,384,256]{2,1,0:T(8,128)(2,1)S(1)}, bf16[2,384,256]{2,1,0:T(8,128)(2,1)}, u32[]{:S(2)}, u32[]{:S(2)}) collective-permute-start(bf16[2,384,256]{2,1,0:T(8,128)(2,1)S(1)} %pad_maximum_fusion.23), channel_id=1, source_target_pairs={{0,4},{4,8},{8,12},{12,0},{1,5},{5,9},{9,13},{13,1},{2,6},{6,10},{... | collective-permute-start | bytes 1179656 | tf_op jit(solution)/shard_map/ppermute | solution.py:169
  252.2 46.9 %collective-permute-start.27 = (bf16[2,384,384]{2,1,0:T(8,128)(2,1)S(1)}, bf16[2,384,384]{2,1,0:T(8,128)(2,1)S(1)}, u32[]{:S(2)}, u32[]{:S(2)}) collective-permute-start(bf16[2,384,384]{2,1,0:T(8,128)(2,1)S(1)} %collective-permute-done.19.refs_2_), channel_id=1, source_target_pairs={{0,16},{16,0},{1,17},{17,1},{2,18},{18,2},{3,19},{19,3},{4,20},{20... | collective-permute-start | bytes 1769480 | tf_op jit(solution)/shard_map/ppermute | solution.py:181
  253.5 56.2 %collective-permute-start.39 = (bf16[2,384,384]{2,1,0:T(8,128)(2,1)S(1)}, bf16[2,384,384]{2,1,0:T(8,128)(2,1)S(1)}, u32[]{:S(2)}, u32[]{:S(2)}) collective-permute-start(bf16[2,384,384]{2,1,0:T(8,128)(2,1)S(1)} %collective-permute-done.37.refs_6_), channel_id=1, source_target_pairs={{0,16},{16,0},{1,17},{17,1},{2,18},{18,2},{3,19},{19,3},{4,20},{20... | collective-permute-start | bytes 1769480 | tf_op jit(solution)/shard_map/ppermute | solution.py:181
  281.7 28.8 %collective-permute-start.35 = (bf16[2,384,384]{2,1,0:T(8,128)(2,1)S(1)}, bf16[2,384,384]{2,1,0:T(8,128)(2,1)S(1)}, u32[]{:S(2)}, u32[]{:S(2)}) collective-permute-start(bf16[2,384,384]{2,1,0:T(8,128)(2,1)S(1)} %collective-permute-done.33.refs_4_), channel_id=1, source_target_pairs={{0,16},{16,0},{1,17},{17,1},{2,18},{18,2},{3,19},{19,3},{4,20},{20... | collective-permute-start | bytes 1769480 | tf_op jit(solution)/shard_map/ppermute | solution.py:181
  283.4 26.3 %collective-permute-start.38 = (bf16[2,384,256]{2,1,0:T(8,128)(2,1)S(1)}, bf16[2,384,256]{2,1,0:T(8,128)(2,1)}, u32[]{:S(2)}, u32[]{:S(2)}) collective-permute-start(bf16[2,384,256]{2,1,0:T(8,128)(2,1)S(1)} %pad_maximum_fusion.25), channel_id=1, source_target_pairs={{0,12},{4,0},{8,4},{12,8},{1,13},{5,1},{9,5},{13,9},{2,14},{6,2},{... | collective-permute-start | bytes 1179656 | tf_op jit(solution)/shard_map/ppermute | solution.py:169
  283.5 27.0 %collective-permute-start.34 = (bf16[2,384,256]{2,1,0:T(8,128)(2,1)S(1)}, bf16[2,384,256]{2,1,0:T(8,128)(2,1)}, u32[]{:S(2)}, u32[]{:S(2)}) collective-permute-start(bf16[2,384,256]{2,1,0:T(8,128)(2,1)S(1)} %pad_maximum_fusion.24), channel_id=1, source_target_pairs={{0,8},{4,12},{8,0},{12,4},{1,9},{5,13},{9,1},{13,5},{2,10},{6,14},... | collective-permute-start | bytes 1179656 | tf_op jit(solution)/shard_map/ppermute | solution.py:169
  299.9 32.5 %collective-permute-start.32 = (bf16[2,384,256]{2,1,0:T(8,128)(2,1)}, bf16[2,384,256]{2,1,0:T(8,128)(2,1)}, u32[]{:S(2)}, u32[]{:S(2)}) collective-permute-start(bf16[2,384,256]{2,1,0:T(8,128)(2,1)} %collective-permute-done.25.refs_2_), channel_id=1, source_target_pairs={{0,16},{16,0},{1,17},{17,1},{2,18},{18,2},{3,19},{19,3},{4,20},{20... | collective-permute-start | bytes 1179656 | tf_op jit(solution)/shard_map/ppermute | solution.py:181
  310.5 21.8 %collective-permute-start.40 = (bf16[2,384,256]{2,1,0:T(8,128)(2,1)}, bf16[2,384,256]{2,1,0:T(8,128)(2,1)}, u32[]{:S(2)}, u32[]{:S(2)}) collective-permute-start(bf16[2,384,256]{2,1,0:T(8,128)(2,1)} %collective-permute-done.38.refs_6_), channel_id=1, source_target_pairs={{0,16},{16,0},{1,17},{17,1},{2,18},{18,2},{3,19},{19,3},{4,20},{20... | collective-permute-start | bytes 1179656 | tf_op jit(solution)/shard_map/ppermute | solution.py:181
  311.4 24.3 %collective-permute-start.36 = (bf16[2,384,256]{2,1,0:T(8,128)(2,1)}, bf16[2,384,256]{2,1,0:T(8,128)(2,1)}, u32[]{:S(2)}, u32[]{:S(2)}) collective-permute-start(bf16[2,384,256]{2,1,0:T(8,128)(2,1)} %collective-permute-done.34.refs_4_), channel_id=1, source_target_pairs={{0,16},{16,0},{1,17},{17,1},{2,18},{18,2},{3,19},{19,3},{4,20},{20... | collective-permute-start | bytes 1179656 | tf_op jit(solution)/shard_map/ppermute | solution.py:181
  346.0 3.8 %collective-permute-start.41 = (f32[2,288,768]{2,1,0:T(8,128)S(1)}, f32[2,288,768]{2,1,0:T(8,128)S(1)}, u32[]{:S(2)}, u32[]{:S(2)}) collective-permute-start(f32[2,288,768]{2,1,0:T(8,128)S(1)} %pad_maximum_fusion.2), channel_id=1, source_target_pairs={{0,1},{1,0},{2,3},{3,2},{4,5},{5,4},{6,7},{7,6},{8,9},{9,8},{10,11... | collective-permute-start | bytes 5308424 | tf_op jit(solution)/shard_map/ppermute | solution.py:266
  350.1 8.3 %collective-permute-start.43 = (bf16[2,72,768]{2,1,0:T(8,128)(2,1)S(1)}, bf16[2,72,768]{2,1,0:T(8,128)(2,1)S(1)}, u32[]{:S(2)}, u32[]{:S(2)}) collective-permute-start(bf16[2,72,768]{2,1,0:T(8,128)(2,1)S(1)} %pad_maximum_fusion.27), channel_id=1, source_target_pairs={{0,2},{1,3},{2,0},{3,1},{4,6},{5,7},{6,4},{7,5},{8,10},{9,11},{10,... | collective-permute-start | bytes 663560 | tf_op jit(solution)/shard_map/ppermute | solution.py:282
  351.7 10.7 %collective-permute-start.42 = (bf16[2,72,768]{2,1,0:T(8,128)(2,1)S(1)}, bf16[2,72,768]{2,1,0:T(8,128)(2,1)S(1)}, u32[]{:S(2)}, u32[]{:S(2)}) collective-permute-start(bf16[2,72,768]{2,1,0:T(8,128)(2,1)S(1)} %pad_maximum_fusion.26), channel_id=1, source_target_pairs={{0,2},{1,3},{2,0},{3,1},{4,6},{5,7},{6,4},{7,5},{8,10},{9,11},{10,... | collective-permute-start | bytes 663560 | tf_op jit(solution)/shard_map/ppermute | solution.py:282
  358.5 7.6 %collective-permute-start.44 = (bf16[72,768]{1,0:T(8,128)(2,1)S(1)}, bf16[72,768]{1,0:T(8,128)(2,1)S(1)}, u32[]{:S(2)}, u32[]{:S(2)}) collective-permute-start(bf16[72,768]{1,0:T(8,128)(2,1)S(1)} %get-tuple-element.160), channel_id=1, source_target_pairs={{0,4},{4,8},{8,12},{12,0},{1,5},{5,9},{9,13},{13,1},{2,6},{6,10},{... | collective-permute-start | bytes 331784 | tf_op jit(solution)/shard_map/ppermute | solution.py:286
  358.6 10.2 %collective-permute-start.45 = (bf16[72,768]{1,0:T(8,128)(2,1)S(1)}, bf16[72,768]{1,0:T(8,128)(2,1)S(1)}, u32[]{:S(2)}, u32[]{:S(2)}) collective-permute-start(bf16[72,768]{1,0:T(8,128)(2,1)S(1)} %get-tuple-element.161), channel_id=1, source_target_pairs={{0,8},{4,12},{8,0},{12,4},{1,9},{5,13},{9,1},{13,5},{2,10},{6,14},... | collective-permute-start | bytes 331784 | tf_op jit(solution)/shard_map/ppermute | solution.py:286
  362.5 6.5 %collective-permute-start.46 = (bf16[72,768]{1,0:T(8,128)(2,1)S(1)}, bf16[72,768]{1,0:T(8,128)(2,1)S(1)}, u32[]{:S(2)}, u32[]{:S(2)}) collective-permute-start(bf16[72,768]{1,0:T(8,128)(2,1)S(1)} %get-tuple-element.159), channel_id=1, source_target_pairs={{0,12},{4,0},{8,4},{12,8},{1,13},{5,1},{9,5},{13,9},{2,14},{6,2},{... | collective-permute-start | bytes 331784 | tf_op jit(solution)/shard_map/ppermute | solution.py:286
  (70 other events, 1471.0 us)

commit v3 on v2

--- a/solution.py
+++ b/solution.py
@@ -48,11 +48,8 @@
 
 def column_chunks(width):
     unit = width // 16
-    sizes = (3, 4, 4, 3, 2)
-    bounds = [0]
-    for size in sizes:
-        bounds.append(bounds[-1] + size * unit)
-    return list(zip(bounds[:-1], bounds[1:]))
+    places = ((0, 3), (6, 4), (10, 4), (3, 3), (14, 2))
+    return [(begin * unit, (begin + size) * unit) for begin, size in places]
 
 
 def expert_kernel(n_part, first, rows_ref, scale_ref, grad_ref, *refs):
@@ -96,6 +93,7 @@
     hidden_part = grad.shape[1]
     depth, width = parts[0].shape[1:]
     tile = 256 if width % 256 == 0 and begin % 256 == 0 else 128
+    tile = width if width < 512 and begin % width == 0 else tile
     tile = tile if width % tile == 0 else width
     offset = begin // tile
     whole = lambda shape: pl.BlockSpec(shape, lambda t: (0, 0))

time: 371 us -> 367 us (0.989)
  Pallas kernels: 57.9 us -> 46.5 us
  waiting for transfers between devices: 198 us -> 205 us
    pallas_call x5, Pallas kernels: 57.9 us -> 46.5 us  [expert_chunk(): pl.pallas_call(functools.partial(expert_kernel, len(parts), carried is No...]
    ppermute x15, waiting for transfers between devices: 144 us -> 149 us  [to_owner(): piece = lax.ppermute(piece, 'expert', shift_by('expert', step))]
  transfers between devices with their start and end apart: 47 -> 47, of which waited for: 18 -> 19; matrix products, arithmetic and copies ran while one was open for 9% -> 9% of each run, Pallas kernels for 14% -> 11%
where the time goes in v3:
time: 367 us
  waiting for transfers between devices  205 us (56%)
  starting transfers between devices  57 us (16%)
  Pallas kernels  46.5 us (13%)
  local copies, waits for them, and re-layouts  37.5 us (10%)
  other arithmetic  16.9 us (5%)
    ppermute x15, waiting for transfers between devices, to_owner(): piece = lax.ppermute(piece, 'expert', shift_by('expert', step))  149 us
    pallas_call x5, Pallas kernels, expert_chunk(): pl.pallas_call(functools.partial(expert_kernel, len(parts), carried is No...  46.5 us
    ppermute x20, waiting for transfers between devices, to_both(): spread[chunk, step] = lax.ppermute(piece, 'dp', shift_by('dp', 1))  36.5 us
    ppermute x20, starting transfers between devices, to_both(): spread[chunk, step] = lax.ppermute(piece, 'dp', shift_by('dp', 1))  31.6 us
    unnamed x150, local copies, waits for them, and re-layouts  19.6 us
    ppermute x15, starting transfers between devices, to_owner(): piece = lax.ppermute(piece, 'expert', shift_by('expert', step))  15.3 us
    dynamic_slice x3, local copies, waits for them, and re-layouts, stored(): lax.dynamic_slice(w, (target, 0, begin), (1, depth, end - begin))[0]  11.9 us
    another operation x20, other arithmetic, stored(): jnp.stack([lax.dynamic_slice(w, (target, 0, begin), (1, depth, end - begi...  11.4 us
  transfers between devices with their start and end apart: 47, of which 19 were waited for; matrix products, arithmetic and copies ran while one was open for 9% of the time, Pallas kernels for 11%

profile of v3, /device:TPU:0, one launch (start us, length us, event | category | flops | bytes accessed | tf_op | source)
XLA Modules:
  0.0 366.6 jit_solution(17616870335710640955)
XLA Ops:
  0.7 5.2 %constant_dynamic-slice_fusion.20 = (bf16[1,384,512]{2,1,0:T(8,128)(2,1)}, bf16[1,384,512]{2,1,0:T(8,128)(2,1)}, bf16[1,384,512]{2,1,0:T(8,128)(2,1)}, bf16[1,38...) fusion(bf16[4,384,2048]{2,1,0:T(8,128)(2,1)} %param.10, ...), kind=kLoop, calls=%fused_computation.109 | loop fusion | bytes 12582928 | tf_op jit(solution)/shard_map/dynamic_slice | solution.py:149
  6.0 3.0 collective-permute-start.9
  12.7 1.6 collective-permute-start
  14.3 2.6 collective-permute-start.1
  16.9 1.3 collective-permute-start.2
  18.2 4.1 %constant_dynamic-slice_fusion.12 = (bf16[1,384,384]{2,1,0:T(8,128)(2,1)}, bf16[1,384,384]{2,1,0:T(8,128)(2,1)}, bf16[1,384,384]{2,1,0:T(8,128)(2,1)}, bf16[1,38...) fusion(bf16[4,384,2048]{2,1,0:T(8,128)(2,1)} %param.10, ...), kind=kLoop, calls=%fused_computation.101 | loop fusion | bytes 9437200 | tf_op jit(solution)/shard_map/dynamic_slice | solution.py:149
  29.7 1.5 collective-permute-start.17
  31.2 1.6 collective-permute-start.6
  34.0 6.0 %collective-permute-done.14.refs_1_ = bf16[2,384,384]{2,1,0:T(8,128)(2,1)S(1)} collective-permute-done((bf16[2,384,384]{2,1,0:T(8,128)(2,1)S(1)}, bf16[2,384,384]{2,1,0:T(8,128)(2,1)S(1)}, u32[]{:S(2)}, u32[]{:S(2)}) %collective-permute-start.14) | collective-permute-done | bytes 589856 | tf_op jit(solution)/shard_map/ppermute | solution.py:179
  40.0 3.2 collective-permute-start.16
  44.1 14.2 %collective-permute-done.6.refs_2_ = bf16[2,384,384]{2,1,0:T(8,128)(2,1)} collective-permute-done((bf16[2,384,384]{2,1,0:T(8,128)(2,1)S(1)}, bf16[2,384,384]{2,1,0:T(8,128)(2,1)}, u32[]{:S(2)}, u32[]{:S(2)}) %collective-permute-start.6) | collective-permute-done | bytes 589856 | tf_op jit(solution)/shard_map/ppermute | solution.py:167
  60.4 2.5 constant_dynamic-slice_fusion.14
  63.0 1.6 collective-permute-start.4
  64.9 16.7 %collective-permute-done.16.refs_4_ = bf16[2,384,384]{2,1,0:T(8,128)(2,1)} collective-permute-done((bf16[2,384,384]{2,1,0:T(8,128)(2,1)}, bf16[2,384,384]{2,1,0:T(8,128)(2,1)}, u32[]{:S(2)}, u32[]{:S(2)}) %collective-permute-start.16) | collective-permute-done | bytes 589856 | tf_op jit(solution)/shard_map/ppermute | solution.py:167
  81.5 1.2 collective-permute-start.15
  86.3 1.3 pad_maximum_fusion.5
  88.4 3.9 %collective-permute-start.23 = (bf16[2,384,512]{2,1,0:T(8,128)(2,1)S(1)}, bf16[2,384,512]{2,1,0:T(8,128)(2,1)S(1)}, u32[]{:S(2)}, u32[]{:S(2)}) collective-permute-start(bf16[2,384,512]{2,1,0:T(8,128)(2,1)S(1)} %copy-done.59), channel_id=1, source_target_pairs={{0,12},{4,0},{8,4},{12,8},{1,13},{5,1},{9,5},{13,9},{2,14},{6,2},{... | collective-permute-start | bytes 2359304 | tf_op jit(solution)/shard_map/ppermute | solution.py:167
  92.2 1.2 collective-permute-start.18
  93.5 1.4 pad_maximum_fusion
  94.9 3.1 collective-permute-done.15.refs_3_
  98.8 11.8 %collective-permute-done.10.refs_7_ = bf16[2,384,384]{2,1,0:T(8,128)(2,1)S(1)} collective-permute-done((bf16[2,384,384]{2,1,0:T(8,128)(2,1)}, bf16[2,384,384]{2,1,0:T(8,128)(2,1)S(1)}, u32[]{:S(2)}, u32[]{:S(2)}) %collective-permute-start.10) | collective-permute-done | bytes 589856 | tf_op jit(solution)/shard_map/ppermute | solution.py:179
  113.8 9.5 %collective-permute-done.18.refs_5_ = bf16[2,384,384]{2,1,0:T(8,128)(2,1)S(1)} collective-permute-done((bf16[2,384,384]{2,1,0:T(8,128)(2,1)}, bf16[2,384,384]{2,1,0:T(8,128)(2,1)S(1)}, u32[]{:S(2)}, u32[]{:S(2)}) %collective-permute-start.18) | collective-permute-done | bytes 589856 | tf_op jit(solution)/shard_map/ppermute | solution.py:179
  126.8 43.2 %collective-permute-done.20.refs_4_ = bf16[2,384,512]{2,1,0:T(8,128)(2,1)S(1)} collective-permute-done((bf16[2,384,512]{2,1,0:T(8,128)(2,1)S(1)}, bf16[2,384,512]{2,1,0:T(8,128)(2,1)S(1)}, u32[]{:S(2)}, u32[]{:S(2)}) %collective-permute-start.20) | collective-permute-done | bytes 786464 | tf_op jit(solution)/shard_map/ppermute | solution.py:167
  174.6 1.2 collective-permute-start.12
  176.6 8.5 %shard_map.77 = (bf16[288,2048]{1,0:T(8,128)(2,1)}, f32[288,3072]{1,0:T(8,128)}, f32[8,128]{1,0:T(8,128)}) custom-call(bf16[288,3072]{1,0:T(8,128)(2,1)} %dynamic-slice_dynamic-update-slice_fusion.rows_ref, f32[288,1]{1,0:T(8,128)S(1)} %maximum_convert_fusion.scale_ref, bf16[288,2048]{1,0:T(8,128)(2,1)S(1)} %bitcast.83, bf16[2,384,384]{2,1,0:T(8,128)(2,1)S(1)} %copy-done.5, ...), custom_call_target="tpu_custom_call" | custom-call | flops 1024 | bytes 1024 | tf_op jit(solution)/shard_map/pallas_call | solution.py:110
  185.1 2.3 collective-permute-start.19
  187.4 3.6 collective-permute-done.30.refs_6_
  193.0 40.8 %collective-permute-done.28.refs_4_ = bf16[2,384,512]{2,1,0:T(8,128)(2,1)S(1)} collective-permute-done((bf16[2,384,512]{2,1,0:T(8,128)(2,1)}, bf16[2,384,512]{2,1,0:T(8,128)(2,1)S(1)}, u32[]{:S(2)}, u32[]{:S(2)}) %collective-permute-start.28) | collective-permute-done | bytes 786464 | tf_op jit(solution)/shard_map/ppermute | solution.py:167
  235.6 1.6 collective-permute-start.33
  237.3 10.7 %shard_map.78 = (bf16[288,2048]{1,0:T(8,128)(2,1)}, f32[288,3072]{1,0:T(8,128)}, f32[8,128]{1,0:T(8,128)}) custom-call(bf16[288,3072]{1,0:T(8,128)(2,1)} %dynamic-slice_dynamic-update-slice_fusion.rows_ref, f32[288,1]{1,0:T(8,128)S(1)} %maximum_convert_fusion.scale_ref, bf16[288,2048]{1,0:T(8,128)(2,1)} %bitcast.81, ...), custom_call_target="tpu_custom_call", output_to_operand_aliasing={{1}: (11, {}), {0}: (12, {})} | custom-call | flops 1024 | bytes 1024 | tf_op jit(solution)/shard_map/pallas_call | solution.py:110
  248.7 2.7 collective-permute-done.37.refs_6_
  251.3 1.2 collective-permute-start.27
  253.4 28.2 %collective-permute-done.33.refs_4_ = bf16[2,384,384]{2,1,0:T(8,128)(2,1)S(1)} collective-permute-done((bf16[2,384,384]{2,1,0:T(8,128)(2,1)S(1)}, bf16[2,384,384]{2,1,0:T(8,128)(2,1)S(1)}, u32[]{:S(2)}, u32[]{:S(2)}) %collective-permute-start.33) | collective-permute-done | bytes 589856 | tf_op jit(solution)/shard_map/ppermute | solution.py:167
  281.6 1.6 collective-permute-start.35
  283.3 1.6 collective-permute-start.34
  284.9 10.5 %shard_map.79 = (bf16[288,2048]{1,0:T(8,128)(2,1)}, f32[288,3072]{1,0:T(8,128)}, f32[8,128]{1,0:T(8,128)}) custom-call(bf16[288,3072]{1,0:T(8,128)(2,1)} %dynamic-slice_dynamic-update-slice_fusion.rows_ref, f32[288,1]{1,0:T(8,128)S(1)} %maximum_convert_fusion.scale_ref, bf16[288,2048]{1,0:T(8,128)(2,1)} %bitcast.82, ...), custom_call_target="tpu_custom_call", output_to_operand_aliasing={{1}: (11, {}), {0}: (12, {})} | custom-call | flops 1024 | bytes 1024 | tf_op jit(solution)/shard_map/pallas_call | solution.py:110
  296.3 9.8 %collective-permute-start.32 = (bf16[2,384,256]{2,1,0:T(8,128)(2,1)}, bf16[2,384,256]{2,1,0:T(8,128)(2,1)}, u32[]{:S(2)}, u32[]{:S(2)}) collective-permute-start(bf16[2,384,256]{2,1,0:T(8,128)(2,1)} %collective-permute-done.25.refs_2_), channel_id=1, source_target_pairs={{0,16},{16,0},{1,17},{17,1},{2,18},{18,2},{3,19},{19,3},{4,20},{20... | collective-permute-start | bytes 1179656 | tf_op jit(solution)/shard_map/ppermute | solution.py:179
  307.8 2.0 collective-permute-start.36
  317.3 9.0 %shard_map.80 = (bf16[288,2048]{1,0:T(8,128)(2,1)}, f32[288,3072]{1,0:T(8,128)}, f32[8,128]{1,0:T(8,128)}) custom-call(bf16[288,3072]{1,0:T(8,128)(2,1)} %dynamic-slice_dynamic-update-slice_fusion.rows_ref, f32[288,1]{1,0:T(8,128)S(1)} %maximum_convert_fusion.scale_ref, ...), custom_call_target="tpu_custom_call", output_to_operand_aliasing={{1}: (11, {}), {0}: (12, {})} | custom-call | flops 1024 | bytes 1024 | tf_op jit(solution)/shard_map/pallas_call | solution.py:110
  326.3 5.8 %collective-permute-done.36.refs_5_ = bf16[2,384,256]{2,1,0:T(8,128)(2,1)} collective-permute-done((bf16[2,384,256]{2,1,0:T(8,128)(2,1)}, bf16[2,384,256]{2,1,0:T(8,128)(2,1)}, u32[]{:S(2)}, u32[]{:S(2)}) %collective-permute-start.36) | collective-permute-done | bytes 393248 | tf_op jit(solution)/shard_map/ppermute | solution.py:179
  332.1 7.8 %shard_map.81 = (bf16[288,2048]{1,0:T(8,128)(2,1)}, f32[288,3072]{1,0:T(8,128)}, f32[8,128]{1,0:T(8,128)}) custom-call(bf16[288,3072]{1,0:T(8,128)(2,1)} %dynamic-slice_dynamic-update-slice_fusion.rows_ref, f32[288,1]{1,0:T(8,128)S(1)} %maximum_convert_fusion.scale_ref, ...), custom_call_target="tpu_custom_call", output_to_operand_aliasing={{1}: (11, {}), {0}: (12, {})} | custom-call | flops 1024 | bytes 1024 | tf_op jit(solution)/shard_map/pallas_call | solution.py:110
  340.0 2.2 constant_dynamic-slice_fusion.3
  342.5 3.7 %collective-permute-done.41 = f32[2,288,768]{2,1,0:T(8,128)S(1)} collective-permute-done((f32[2,288,768]{2,1,0:T(8,128)S(1)}, f32[2,288,768]{2,1,0:T(8,128)S(1)}, u32[]{:S(2)}, u32[]{:S(2)}) %collective-permute-start.41) | collective-permute-done | bytes 1769504 | tf_op jit(solution)/shard_map/ppermute | solution.py:264
  346.5 1.6 collective-permute-start.43
  348.9 5.9 %collective-permute-done.43 = bf16[2,72,768]{2,1,0:T(8,128)(2,1)S(1)} collective-permute-done((bf16[2,72,768]{2,1,0:T(8,128)(2,1)S(1)}, bf16[2,72,768]{2,1,0:T(8,128)(2,1)S(1)}, u32[]{:S(2)}, u32[]{:S(2)}) %collective-permute-start.43) | collective-permute-done | bytes 221216 | tf_op jit(solution)/shard_map/ppermute | solution.py:280
  355.4 3.4 collective-permute-done.42
  359.0 3.5 collective-permute-done.44
  362.5 2.7 collective-permute-done.45
  (270 shorter events, 51.4 us)
Async XLA Ops:
  6.0 76.8 %collective-permute-start.9 = (bf16[2,384,512]{2,1,0:T(8,128)(2,1)S(1)}, bf16[2,384,512]{2,1,0:T(8,128)(2,1)}, u32[]{:S(2)}, u32[]{:S(2)}) collective-permute-start(bf16[2,384,512]{2,1,0:T(8,128)(2,1)S(1)} %pad_maximum_fusion.4.refs_0_), channel_id=1, source_target_pairs={{0,16},{16,0},{1,17},{17,1},{2,18},{18,2},{3,19},{19,3},{4,20},{20... | collective-permute-start | bytes 2359304 | tf_op jit(solution)/shard_map/ppermute | solution.py:179
  12.7 16.5 %collective-permute-start = (bf16[72,896]{1,0:T(8,128)(2,1)}, bf16[72,896]{1,0:T(8,128)(2,1)S(1)}, u32[]{:S(2)}, u32[]{:S(2)}) collective-permute-start(bf16[72,896]{1,0:T(8,128)(2,1)} %get-tuple-element.153), channel_id=1, source_target_pairs={{0,4},{4,8},{8,12},{12,0},{1,5},{5,9},{9,13},{13,1},{2,6},{6,10},{... | collective-permute-start | bytes 387080 | tf_op jit(solution)/shard_map/ppermute | solution.py:215
  14.3 15.4 %collective-permute-start.1 = (bf16[72,896]{1,0:T(8,128)(2,1)}, bf16[72,896]{1,0:T(8,128)(2,1)S(1)}, u32[]{:S(2)}, u32[]{:S(2)}) collective-permute-start(bf16[72,896]{1,0:T(8,128)(2,1)} %get-tuple-element.152), channel_id=1, source_target_pairs={{0,8},{4,12},{8,0},{12,4},{1,9},{5,13},{9,1},{13,5},{2,10},{6,14},... | collective-permute-start | bytes 387080 | tf_op jit(solution)/shard_map/ppermute | solution.py:215
  16.9 14.3 %collective-permute-start.2 = (bf16[72,896]{1,0:T(8,128)(2,1)}, bf16[72,896]{1,0:T(8,128)(2,1)}, u32[]{:S(2)}, u32[]{:S(2)}) collective-permute-start(bf16[72,896]{1,0:T(8,128)(2,1)} %get-tuple-element.151), channel_id=1, source_target_pairs={{0,12},{4,0},{8,4},{12,8},{1,13},{5,1},{9,5},{13,9},{2,14},{6,2},{... | collective-permute-start | bytes 387080 | tf_op jit(solution)/shard_map/ppermute | solution.py:215
  22.5 17.5 %collective-permute-start.14 = (bf16[2,384,384]{2,1,0:T(8,128)(2,1)S(1)}, bf16[2,384,384]{2,1,0:T(8,128)(2,1)S(1)}, u32[]{:S(2)}, u32[]{:S(2)}) collective-permute-start(bf16[2,384,384]{2,1,0:T(8,128)(2,1)S(1)} %pad_maximum_fusion.14.refs_0_), channel_id=1, source_target_pairs={{0,16},{16,0},{1,17},{17,1},{2,18},{18,2},{3,19},{19,3},{4,20},{20... | collective-permute-start | bytes 1769480 | tf_op jit(solution)/shard_map/ppermute | solution.py:179
  29.2 35.4 %collective-permute-start.8 = (bf16[2,384,384]{2,1,0:T(8,128)(2,1)}, bf16[2,384,384]{2,1,0:T(8,128)(2,1)}, u32[]{:S(2)}, u32[]{:S(2)}) collective-permute-start(bf16[2,384,384]{2,1,0:T(8,128)(2,1)} %pad_maximum_fusion.12), channel_id=1, source_target_pairs={{0,12},{4,0},{8,4},{12,8},{1,13},{5,1},{9,5},{13,9},{2,14},{6,2},{... | collective-permute-start | bytes 1769480 | tf_op jit(solution)/shard_map/ppermute | solution.py:167
  29.7 54.0 %collective-permute-start.17 = (bf16[2,384,512]{2,1,0:T(8,128)(2,1)S(1)}, bf16[2,384,512]{2,1,0:T(8,128)(2,1)S(1)}, u32[]{:S(2)}, u32[]{:S(2)}) collective-permute-start(bf16[2,384,512]{2,1,0:T(8,128)(2,1)S(1)} %pad_maximum_fusion.6.refs_0_), channel_id=1, source_target_pairs={{0,16},{16,0},{1,17},{17,1},{2,18},{18,2},{3,19},{19,3},{4,20},{20... | collective-permute-start | bytes 2359304 | tf_op jit(solution)/shard_map/ppermute | solution.py:179
  31.2 27.1 %collective-permute-start.6 = (bf16[2,384,384]{2,1,0:T(8,128)(2,1)S(1)}, bf16[2,384,384]{2,1,0:T(8,128)(2,1)}, u32[]{:S(2)}, u32[]{:S(2)}) collective-permute-start(bf16[2,384,384]{2,1,0:T(8,128)(2,1)S(1)} %pad_maximum_fusion.11), channel_id=1, source_target_pairs={{0,4},{4,8},{8,12},{12,0},{1,5},{5,9},{9,13},{13,1},{2,6},{6,10},{... | collective-permute-start | bytes 1769480 | tf_op jit(solution)/shard_map/ppermute | solution.py:167
  40.0 41.5 %collective-permute-start.16 = (bf16[2,384,384]{2,1,0:T(8,128)(2,1)}, bf16[2,384,384]{2,1,0:T(8,128)(2,1)}, u32[]{:S(2)}, u32[]{:S(2)}) collective-permute-start(bf16[2,384,384]{2,1,0:T(8,128)(2,1)} %pad_maximum_fusion.15), channel_id=1, source_target_pairs={{0,8},{4,12},{8,0},{12,4},{1,9},{5,13},{9,1},{13,5},{2,10},{6,14},... | collective-permute-start | bytes 1769480 | tf_op jit(solution)/shard_map/ppermute | solution.py:167
  58.3 4.6 %collective-permute-start.3 = (bf16[288,768]{1,0:T(8,128)(2,1)}, bf16[288,768]{1,0:T(8,128)(2,1)S(1)}, u32[]{:S(2)}, u32[]{:S(2)}) collective-permute-start(bf16[288,768]{1,0:T(8,128)(2,1)} %get-tuple-element.145), channel_id=1, source_target_pairs={{0,1},{1,0},{2,3},{3,2},{4,5},{5,4},{6,7},{7,6},{8,9},{9,8},{10,11... | collective-permute-start | bytes 1327112 | tf_op jit(solution)/shard_map/ppermute | solution.py:45
  63.0 25.4 %collective-permute-start.4 = (bf16[288,768]{1,0:T(8,128)(2,1)}, bf16[288,768]{1,0:T(8,128)(2,1)}, u32[]{:S(2)}, u32[]{:S(2)}) collective-permute-start(bf16[288,768]{1,0:T(8,128)(2,1)} %get-tuple-element.145), channel_id=1, source_target_pairs={{0,2},{1,3},{2,0},{3,1},{4,6},{5,7},{6,4},{7,5},{8,10},{9,11},{10,... | collective-permute-start | bytes 1327112 | tf_op jit(solution)/shard_map/ppermute | solution.py:45
  64.6 27.7 %collective-permute-start.5 = (bf16[288,768]{1,0:T(8,128)(2,1)}, bf16[288,768]{1,0:T(8,128)(2,1)}, u32[]{:S(2)}, u32[]{:S(2)}) collective-permute-start(bf16[288,768]{1,0:T(8,128)(2,1)} %get-tuple-element.145), channel_id=1, source_target_pairs={{0,3},{1,2},{2,1},{3,0},{4,7},{5,6},{6,5},{7,4},{8,11},{9,10},{10,... | collective-permute-start | bytes 1327112 | tf_op jit(solution)/shard_map/ppermute | solution.py:45
  81.5 16.5 %collective-permute-start.15 = (bf16[2,384,384]{2,1,0:T(8,128)(2,1)}, bf16[2,384,384]{2,1,0:T(8,128)(2,1)S(1)}, u32[]{:S(2)}, u32[]{:S(2)}) collective-permute-start(bf16[2,384,384]{2,1,0:T(8,128)(2,1)} %collective-permute-done.6.refs_2_), channel_id=1, source_target_pairs={{0,16},{16,0},{1,17},{17,1},{2,18},{18,2},{3,19},{19,3},{4,20},{20... | collective-permute-start | bytes 1769480 | tf_op jit(solution)/shard_map/ppermute | solution.py:179
  82.8 29.9 %collective-permute-start.7 = (bf16[2,384,512]{2,1,0:T(8,128)(2,1)}, bf16[2,384,512]{2,1,0:T(8,128)(2,1)}, u32[]{:S(2)}, u32[]{:S(2)}) collective-permute-start(bf16[2,384,512]{2,1,0:T(8,128)(2,1)} %pad_maximum_fusion.3), channel_id=1, source_target_pairs={{0,4},{4,8},{8,12},{12,0},{1,5},{5,9},{9,13},{13,1},{2,6},{6,10},{... | collective-permute-start | bytes 2359304 | tf_op jit(solution)/shard_map/ppermute | solution.py:167
  84.7 26.0 %collective-permute-start.10 = (bf16[2,384,384]{2,1,0:T(8,128)(2,1)}, bf16[2,384,384]{2,1,0:T(8,128)(2,1)S(1)}, u32[]{:S(2)}, u32[]{:S(2)}) collective-permute-start(bf16[2,384,384]{2,1,0:T(8,128)(2,1)} %collective-permute-done.8.refs_6_), channel_id=1, source_target_pairs={{0,16},{16,0},{1,17},{17,1},{2,18},{18,2},{3,19},{19,3},{4,20},{20... | collective-permute-start | bytes 1769480 | tf_op jit(solution)/shard_map/ppermute | solution.py:179
  88.4 35.7 %collective-permute-start.23 = (bf16[2,384,512]{2,1,0:T(8,128)(2,1)S(1)}, bf16[2,384,512]{2,1,0:T(8,128)(2,1)S(1)}, u32[]{:S(2)}, u32[]{:S(2)}) collective-permute-start(bf16[2,384,512]{2,1,0:T(8,128)(2,1)S(1)} %copy-done.59), channel_id=1, source_target_pairs={{0,12},{4,0},{8,4},{12,8},{1,13},{5,1},{9,5},{13,9},{2,14},{6,2},{... | collective-permute-start | bytes 2359304 | tf_op jit(solution)/shard_map/ppermute | solution.py:167
  92.2 31.0 %collective-permute-start.18 = (bf16[2,384,384]{2,1,0:T(8,128)(2,1)}, bf16[2,384,384]{2,1,0:T(8,128)(2,1)S(1)}, u32[]{:S(2)}, u32[]{:S(2)}) collective-permute-start(bf16[2,384,384]{2,1,0:T(8,128)(2,1)} %collective-permute-done.16.refs_4_), channel_id=1, source_target_pairs={{0,16},{16,0},{1,17},{17,1},{2,18},{18,2},{3,19},{19,3},{4,20},{20... | collective-permute-start | bytes 1769480 | tf_op jit(solution)/shard_map/ppermute | solution.py:179
  98.0 72.0 %collective-permute-start.20 = (bf16[2,384,512]{2,1,0:T(8,128)(2,1)S(1)}, bf16[2,384,512]{2,1,0:T(8,128)(2,1)S(1)}, u32[]{:S(2)}, u32[]{:S(2)}) collective-permute-start(bf16[2,384,512]{2,1,0:T(8,128)(2,1)S(1)} %copy-done.58), channel_id=1, source_target_pairs={{0,8},{4,12},{8,0},{12,4},{1,9},{5,13},{9,1},{13,5},{2,10},{6,14},... | collective-permute-start | bytes 2359304 | tf_op jit(solution)/shard_map/ppermute | solution.py:167
  111.5 59.3 %collective-permute-start.21 = (bf16[2,384,384]{2,1,0:T(8,128)(2,1)S(1)}, bf16[2,384,384]{2,1,0:T(8,128)(2,1)S(1)}, u32[]{:S(2)}, u32[]{:S(2)}) collective-permute-start(bf16[2,384,384]{2,1,0:T(8,128)(2,1)S(1)} %pad_maximum_fusion.16.refs_0_), channel_id=1, source_target_pairs={{0,16},{16,0},{1,17},{17,1},{2,18},{18,2},{3,19},{19,3},{4,20},{20... | collective-permute-start | bytes 1769480 | tf_op jit(solution)/shard_map/ppermute | solution.py:179
  112.7 58.9 %collective-permute-start.11 = (bf16[2,384,512]{2,1,0:T(8,128)(2,1)}, bf16[2,384,512]{2,1,0:T(8,128)(2,1)S(1)}, u32[]{:S(2)}, u32[]{:S(2)}) collective-permute-start(bf16[2,384,512]{2,1,0:T(8,128)(2,1)} %collective-permute-done.7.refs_2_), channel_id=1, source_target_pairs={{0,16},{16,0},{1,17},{17,1},{2,18},{18,2},{3,19},{19,3},{4,20},{20... | collective-permute-start | bytes 2359304 | tf_op jit(solution)/shard_map/ppermute | solution.py:179
  113.5 63.1 %copy-start.29 = (bf16[2,384,384]{2,1,0:T(8,128)(2,1)S(1)}, bf16[2,384,384]{2,1,0:T(8,128)(2,1)}, u32[]{:S(2)}) copy-start(bf16[2,384,384]{2,1,0:T(8,128)(2,1)} %copy-done.28) | copy-start | bytes 1769476
  123.3 51.3 %collective-permute-start.13 = (bf16[2,384,512]{2,1,0:T(8,128)(2,1)S(1)}, bf16[2,384,512]{2,1,0:T(8,128)(2,1)S(1)}, u32[]{:S(2)}, u32[]{:S(2)}) collective-permute-start(bf16[2,384,512]{2,1,0:T(8,128)(2,1)S(1)} %pad_maximum_fusion.5), channel_id=1, source_target_pairs={{0,4},{4,8},{8,12},{12,0},{1,5},{5,9},{9,13},{13,1},{2,6},{6,10},{... | collective-permute-start | bytes 2359304 | tf_op jit(solution)/shard_map/ppermute | solution.py:167
  124.1 61.1 %collective-permute-start.24 = (bf16[2,384,512]{2,1,0:T(8,128)(2,1)S(1)}, bf16[2,384,512]{2,1,0:T(8,128)(2,1)}, u32[]{:S(2)}, u32[]{:S(2)}) collective-permute-start(bf16[2,384,512]{2,1,0:T(8,128)(2,1)S(1)} %collective-permute-done.23.refs_6_), channel_id=1, source_target_pairs={{0,16},{16,0},{1,17},{17,1},{2,18},{18,2},{3,19},{19,3},{4,20},{20... | collective-permute-start | bytes 2359304 | tf_op jit(solution)/shard_map/ppermute | solution.py:179
  170.0 21.0 %collective-permute-start.30 = (bf16[2,384,512]{2,1,0:T(8,128)(2,1)}, bf16[2,384,512]{2,1,0:T(8,128)(2,1)S(1)}, u32[]{:S(2)}, u32[]{:S(2)}) collective-permute-start(bf16[2,384,512]{2,1,0:T(8,128)(2,1)} %pad_maximum_fusion.10), channel_id=1, source_target_pairs={{0,12},{4,0},{8,4},{12,8},{1,13},{5,1},{9,5},{13,9},{2,14},{6,2},{... | collective-permute-start | bytes 2359304 | tf_op jit(solution)/shard_map/ppermute | solution.py:167
  171.6 62.2 %collective-permute-start.28 = (bf16[2,384,512]{2,1,0:T(8,128)(2,1)}, bf16[2,384,512]{2,1,0:T(8,128)(2,1)S(1)}, u32[]{:S(2)}, u32[]{:S(2)}) collective-permute-start(bf16[2,384,512]{2,1,0:T(8,128)(2,1)} %pad_maximum_fusion.9), channel_id=1, source_target_pairs={{0,8},{4,12},{8,0},{12,4},{1,9},{5,13},{9,1},{13,5},{2,10},{6,14},... | collective-permute-start | bytes 2359304 | tf_op jit(solution)/shard_map/ppermute | solution.py:167
  171.6 20.4 %collective-permute-start.22 = (bf16[2,384,512]{2,1,0:T(8,128)(2,1)S(1)}, bf16[2,384,512]{2,1,0:T(8,128)(2,1)S(1)}, u32[]{:S(2)}, u32[]{:S(2)}) collective-permute-start(bf16[2,384,512]{2,1,0:T(8,128)(2,1)S(1)} %collective-permute-done.20.refs_4_), channel_id=1, source_target_pairs={{0,16},{16,0},{1,17},{17,1},{2,18},{18,2},{3,19},{19,3},{4,20},{20... | collective-permute-start | bytes 2359304 | tf_op jit(solution)/shard_map/ppermute | solution.py:179
  174.6 59.3 %collective-permute-start.12 = (bf16[2,384,256]{2,1,0:T(8,128)(2,1)S(1)}, bf16[2,384,256]{2,1,0:T(8,128)(2,1)S(1)}, u32[]{:S(2)}, u32[]{:S(2)}) collective-permute-start(bf16[2,384,256]{2,1,0:T(8,128)(2,1)S(1)} %copy-done.6), channel_id=1, source_target_pairs={{0,16},{16,0},{1,17},{17,1},{2,18},{18,2},{3,19},{19,3},{4,20},{20... | collective-permute-start | bytes 1179656 | tf_op jit(solution)/shard_map/ppermute | solution.py:179
  185.1 50.5 %collective-permute-start.19 = (bf16[2,384,384]{2,1,0:T(8,128)(2,1)}, bf16[2,384,384]{2,1,0:T(8,128)(2,1)S(1)}, u32[]{:S(2)}, u32[]{:S(2)}) collective-permute-start(bf16[2,384,384]{2,1,0:T(8,128)(2,1)} %pad_maximum_fusion.13), channel_id=1, source_target_pairs={{0,4},{4,8},{8,12},{12,0},{1,5},{5,9},{9,13},{13,1},{2,6},{6,10},{... | collective-permute-start | bytes 1769480 | tf_op jit(solution)/shard_map/ppermute | solution.py:167
  190.9 57.1 %collective-permute-start.26 = (bf16[2,384,512]{2,1,0:T(8,128)(2,1)S(1)}, bf16[2,384,512]{2,1,0:T(8,128)(2,1)S(1)}, u32[]{:S(2)}, u32[]{:S(2)}) collective-permute-start(bf16[2,384,512]{2,1,0:T(8,128)(2,1)S(1)} %collective-permute-done.13.refs_2_), channel_id=1, source_target_pairs={{0,16},{16,0},{1,17},{17,1},{2,18},{18,2},{3,19},{19,3},{4,20},{20... | collective-permute-start | bytes 2359304 | tf_op jit(solution)/shard_map/ppermute | solution.py:179
  192.0 60.6 %collective-permute-start.31 = (bf16[2,384,512]{2,1,0:T(8,128)(2,1)S(1)}, bf16[2,384,512]{2,1,0:T(8,128)(2,1)S(1)}, u32[]{:S(2)}, u32[]{:S(2)}) collective-permute-start(bf16[2,384,512]{2,1,0:T(8,128)(2,1)S(1)} %collective-permute-done.30.refs_6_), channel_id=1, source_target_pairs={{0,16},{16,0},{1,17},{17,1},{2,18},{18,2},{3,19},{19,3},{4,20},{20... | collective-permute-start | bytes 2359304 | tf_op jit(solution)/shard_map/ppermute | solution.py:179
  234.6 47.0 %collective-permute-start.29 = (bf16[2,384,512]{2,1,0:T(8,128)(2,1)S(1)}, bf16[2,384,512]{2,1,0:T(8,128)(2,1)S(1)}, u32[]{:S(2)}, u32[]{:S(2)}) collective-permute-start(bf16[2,384,512]{2,1,0:T(8,128)(2,1)S(1)} %collective-permute-done.28.refs_4_), channel_id=1, source_target_pairs={{0,16},{16,0},{1,17},{17,1},{2,18},{18,2},{3,19},{19,3},{4,20},{20... | collective-permute-start | bytes 2359304 | tf_op jit(solution)/shard_map/ppermute | solution.py:179
  235.4 15.9 %collective-permute-start.37 = (bf16[2,384,384]{2,1,0:T(8,128)(2,1)S(1)}, bf16[2,384,384]{2,1,0:T(8,128)(2,1)S(1)}, u32[]{:S(2)}, u32[]{:S(2)}) collective-permute-start(bf16[2,384,384]{2,1,0:T(8,128)(2,1)S(1)} %pad_maximum_fusion.18), channel_id=1, source_target_pairs={{0,12},{4,0},{8,4},{12,8},{1,13},{5,1},{9,5},{13,9},{2,14},{6,2},{... | collective-permute-start | bytes 1769480 | tf_op jit(solution)/shard_map/ppermute | solution.py:167
  235.6 45.9 %collective-permute-start.33 = (bf16[2,384,384]{2,1,0:T(8,128)(2,1)S(1)}, bf16[2,384,384]{2,1,0:T(8,128)(2,1)S(1)}, u32[]{:S(2)}, u32[]{:S(2)}) collective-permute-start(bf16[2,384,384]{2,1,0:T(8,128)(2,1)S(1)} %pad_maximum_fusion.17), channel_id=1, source_target_pairs={{0,8},{4,12},{8,0},{12,4},{1,9},{5,13},{9,1},{13,5},{2,10},{6,14},... | collective-permute-start | bytes 1769480 | tf_op jit(solution)/shard_map/ppermute | solution.py:167
  248.0 35.3 %collective-permute-start.25 = (bf16[2,384,256]{2,1,0:T(8,128)(2,1)S(1)}, bf16[2,384,256]{2,1,0:T(8,128)(2,1)}, u32[]{:S(2)}, u32[]{:S(2)}) collective-permute-start(bf16[2,384,256]{2,1,0:T(8,128)(2,1)S(1)} %pad_maximum_fusion.23), channel_id=1, source_target_pairs={{0,4},{4,8},{8,12},{12,0},{1,5},{5,9},{9,13},{13,1},{2,6},{6,10},{... | collective-permute-start | bytes 1179656 | tf_op jit(solution)/shard_map/ppermute | solution.py:167
  251.3 44.1 %collective-permute-start.27 = (bf16[2,384,384]{2,1,0:T(8,128)(2,1)S(1)}, bf16[2,384,384]{2,1,0:T(8,128)(2,1)S(1)}, u32[]{:S(2)}, u32[]{:S(2)}) collective-permute-start(bf16[2,384,384]{2,1,0:T(8,128)(2,1)S(1)} %collective-permute-done.19.refs_2_), channel_id=1, source_target_pairs={{0,16},{16,0},{1,17},{17,1},{2,18},{18,2},{3,19},{19,3},{4,20},{20... | collective-permute-start | bytes 1769480 | tf_op jit(solution)/shard_map/ppermute | solution.py:179
  252.6 53.4 %collective-permute-start.39 = (bf16[2,384,384]{2,1,0:T(8,128)(2,1)S(1)}, bf16[2,384,384]{2,1,0:T(8,128)(2,1)S(1)}, u32[]{:S(2)}, u32[]{:S(2)}) collective-permute-start(bf16[2,384,384]{2,1,0:T(8,128)(2,1)S(1)} %collective-permute-done.37.refs_6_), channel_id=1, source_target_pairs={{0,16},{16,0},{1,17},{17,1},{2,18},{18,2},{3,19},{19,3},{4,20},{20... | collective-permute-start | bytes 1769480 | tf_op jit(solution)/shard_map/ppermute | solution.py:179
  281.6 25.4 %collective-permute-start.35 = (bf16[2,384,384]{2,1,0:T(8,128)(2,1)S(1)}, bf16[2,384,384]{2,1,0:T(8,128)(2,1)S(1)}, u32[]{:S(2)}, u32[]{:S(2)}) collective-permute-start(bf16[2,384,384]{2,1,0:T(8,128)(2,1)S(1)} %collective-permute-done.33.refs_4_), channel_id=1, source_target_pairs={{0,16},{16,0},{1,17},{17,1},{2,18},{18,2},{3,19},{19,3},{4,20},{20... | collective-permute-start | bytes 1769480 | tf_op jit(solution)/shard_map/ppermute | solution.py:179
  283.2 22.8 %collective-permute-start.38 = (bf16[2,384,256]{2,1,0:T(8,128)(2,1)S(1)}, bf16[2,384,256]{2,1,0:T(8,128)(2,1)}, u32[]{:S(2)}, u32[]{:S(2)}) collective-permute-start(bf16[2,384,256]{2,1,0:T(8,128)(2,1)S(1)} %pad_maximum_fusion.25), channel_id=1, source_target_pairs={{0,12},{4,0},{8,4},{12,8},{1,13},{5,1},{9,5},{13,9},{2,14},{6,2},{... | collective-permute-start | bytes 1179656 | tf_op jit(solution)/shard_map/ppermute | solution.py:167
  283.3 23.6 %collective-permute-start.34 = (bf16[2,384,256]{2,1,0:T(8,128)(2,1)S(1)}, bf16[2,384,256]{2,1,0:T(8,128)(2,1)}, u32[]{:S(2)}, u32[]{:S(2)}) collective-permute-start(bf16[2,384,256]{2,1,0:T(8,128)(2,1)S(1)} %pad_maximum_fusion.24), channel_id=1, source_target_pairs={{0,8},{4,12},{8,0},{12,4},{1,9},{5,13},{9,1},{13,5},{2,10},{6,14},... | collective-permute-start | bytes 1179656 | tf_op jit(solution)/shard_map/ppermute | solution.py:167
  296.3 30.0 %collective-permute-start.32 = (bf16[2,384,256]{2,1,0:T(8,128)(2,1)}, bf16[2,384,256]{2,1,0:T(8,128)(2,1)}, u32[]{:S(2)}, u32[]{:S(2)}) collective-permute-start(bf16[2,384,256]{2,1,0:T(8,128)(2,1)} %collective-permute-done.25.refs_2_), channel_id=1, source_target_pairs={{0,16},{16,0},{1,17},{17,1},{2,18},{18,2},{3,19},{19,3},{4,20},{20... | collective-permute-start | bytes 1179656 | tf_op jit(solution)/shard_map/ppermute | solution.py:179
  306.9 19.4 %collective-permute-start.40 = (bf16[2,384,256]{2,1,0:T(8,128)(2,1)}, bf16[2,384,256]{2,1,0:T(8,128)(2,1)}, u32[]{:S(2)}, u32[]{:S(2)}) collective-permute-start(bf16[2,384,256]{2,1,0:T(8,128)(2,1)} %collective-permute-done.38.refs_6_), channel_id=1, source_target_pairs={{0,16},{16,0},{1,17},{17,1},{2,18},{18,2},{3,19},{19,3},{4,20},{20... | collective-permute-start | bytes 1179656 | tf_op jit(solution)/shard_map/ppermute | solution.py:179
  307.8 24.3 %collective-permute-start.36 = (bf16[2,384,256]{2,1,0:T(8,128)(2,1)}, bf16[2,384,256]{2,1,0:T(8,128)(2,1)}, u32[]{:S(2)}, u32[]{:S(2)}) collective-permute-start(bf16[2,384,256]{2,1,0:T(8,128)(2,1)} %collective-permute-done.34.refs_4_), channel_id=1, source_target_pairs={{0,16},{16,0},{1,17},{17,1},{2,18},{18,2},{3,19},{19,3},{4,20},{20... | collective-permute-start | bytes 1179656 | tf_op jit(solution)/shard_map/ppermute | solution.py:179
  342.4 3.8 %collective-permute-start.41 = (f32[2,288,768]{2,1,0:T(8,128)S(1)}, f32[2,288,768]{2,1,0:T(8,128)S(1)}, u32[]{:S(2)}, u32[]{:S(2)}) collective-permute-start(f32[2,288,768]{2,1,0:T(8,128)S(1)} %pad_maximum_fusion.2), channel_id=1, source_target_pairs={{0,1},{1,0},{2,3},{3,2},{4,5},{5,4},{6,7},{7,6},{8,9},{9,8},{10,11... | collective-permute-start | bytes 5308424 | tf_op jit(solution)/shard_map/ppermute | solution.py:264
  346.5 8.3 %collective-permute-start.43 = (bf16[2,72,768]{2,1,0:T(8,128)(2,1)S(1)}, bf16[2,72,768]{2,1,0:T(8,128)(2,1)S(1)}, u32[]{:S(2)}, u32[]{:S(2)}) collective-permute-start(bf16[2,72,768]{2,1,0:T(8,128)(2,1)S(1)} %pad_maximum_fusion.27), channel_id=1, source_target_pairs={{0,2},{1,3},{2,0},{3,1},{4,6},{5,7},{6,4},{7,5},{8,10},{9,11},{10,... | collective-permute-start | bytes 663560 | tf_op jit(solution)/shard_map/ppermute | solution.py:280
  348.1 10.7 %collective-permute-start.42 = (bf16[2,72,768]{2,1,0:T(8,128)(2,1)S(1)}, bf16[2,72,768]{2,1,0:T(8,128)(2,1)S(1)}, u32[]{:S(2)}, u32[]{:S(2)}) collective-permute-start(bf16[2,72,768]{2,1,0:T(8,128)(2,1)S(1)} %pad_maximum_fusion.26), channel_id=1, source_target_pairs={{0,2},{1,3},{2,0},{3,1},{4,6},{5,7},{6,4},{7,5},{8,10},{9,11},{10,... | collective-permute-start | bytes 663560 | tf_op jit(solution)/shard_map/ppermute | solution.py:280
  354.9 7.6 %collective-permute-start.44 = (bf16[72,768]{1,0:T(8,128)(2,1)S(1)}, bf16[72,768]{1,0:T(8,128)(2,1)S(1)}, u32[]{:S(2)}, u32[]{:S(2)}) collective-permute-start(bf16[72,768]{1,0:T(8,128)(2,1)S(1)} %get-tuple-element.160), channel_id=1, source_target_pairs={{0,4},{4,8},{8,12},{12,0},{1,5},{5,9},{9,13},{13,1},{2,6},{6,10},{... | collective-permute-start | bytes 331784 | tf_op jit(solution)/shard_map/ppermute | solution.py:284
  355.0 10.2 %collective-permute-start.45 = (bf16[72,768]{1,0:T(8,128)(2,1)S(1)}, bf16[72,768]{1,0:T(8,128)(2,1)S(1)}, u32[]{:S(2)}, u32[]{:S(2)}) collective-permute-start(bf16[72,768]{1,0:T(8,128)(2,1)S(1)} %get-tuple-element.161), channel_id=1, source_target_pairs={{0,8},{4,12},{8,0},{12,4},{1,9},{5,13},{9,1},{13,5},{2,10},{6,14},... | collective-permute-start | bytes 331784 | tf_op jit(solution)/shard_map/ppermute | solution.py:284
  358.9 6.5 %collective-permute-start.46 = (bf16[72,768]{1,0:T(8,128)(2,1)S(1)}, bf16[72,768]{1,0:T(8,128)(2,1)S(1)}, u32[]{:S(2)}, u32[]{:S(2)}) collective-permute-start(bf16[72,768]{1,0:T(8,128)(2,1)S(1)} %get-tuple-element.159), channel_id=1, source_target_pairs={{0,12},{4,0},{8,4},{12,8},{1,13},{5,1},{9,5},{13,9},{2,14},{6,2},{... | collective-permute-start | bytes 331784 | tf_op jit(solution)/shard_map/ppermute | solution.py:284
  (70 other events, 1467.7 us)
